TPU v7x, 32 devices: a whole 2x2x4 slice. The times are simulated.
32 devices in a mesh: dp: 8 (over z, y), mp: 4 (over x, core).
Axes of the slice: x: 2, y: 2, z: 4, core: 2. Of those that a mesh axis runs over, the one named last changes fastest.
Arguments:
- token_ids: int32 [4096], P('dp'), may hold values from 0 to 127
- prefix_lengths: int32 [8], P('dp'), may hold values from 1 to 511
- cluster_ids: int32 [8], replicated, may hold values from 0 to 3
- embedding: bfloat16 [128, 2048], replicated, may hold values from -6 to 6
- w_query: bfloat16 [2048, 2048], P(None, 'mp'), may hold values from -0.125 to 0.125
- w_key: bfloat16 [2048, 2048], P(None, 'mp'), may hold values from -0.125 to 0.125
- w_value: bfloat16 [2048, 2048], P(None, 'mp'), may hold values from -0.125 to 0.125
- w_dense: bfloat16 [2048, 2048], P(None, 'mp'), may hold values from -6 to 6
- w_gate: bfloat16 [2048, 5472], P(None, 'mp'), may hold values from -0.125 to 0.125
- w_up: bfloat16 [2048, 5472], P(None, 'mp'), may hold values from -0.125 to 0.125
- w_down: bfloat16 [2048, 5472], P(None, 'mp'), may hold values from -0.75 to 0.75
- norm1_gain: float32 [2048], replicated, may hold values from 0.5 to 1.5
- norm1_bias: float32 [2048], replicated, may hold values from -4 to 4
- norm2_gain: float32 [2048], replicated, may hold values from 0.5 to 1.5
- norm2_bias: float32 [2048], replicated, may hold values from -4 to 4
- cotangent: bfloat16 [4096, 2048], P('dp'), may hold values from -6 to 6
Outputs:
- block_out: bfloat16 [4096, 2048], P('dp')
- grad_embedding: float32 [128, 2048], P('dp')
- grad_w_query: float32 [2048, 2048], P('dp', 'mp')
- grad_w_key: float32 [2048, 2048], P('dp', 'mp')
- grad_w_value: float32 [2048, 2048], P('dp', 'mp')
- grad_w_dense: float32 [2048, 2048], P('dp', 'mp')
- grad_w_gate: float32 [2048, 5472], P('dp', 'mp')
- grad_w_up: float32 [2048, 5472], P('dp', 'mp')
- grad_w_down: float32 [2048, 5472], P('dp', 'mp')
- grad_norm1_gain: float32 [2048], P('dp')
- grad_norm1_bias: float32 [2048], P('dp')
- grad_norm2_gain: float32 [2048], P('dp')
- grad_norm2_bias: float32 [2048], P('dp')
All inputs are finite; a program needn't handle non-finite values.
Results may differ from a plain program's by a relative error of at most 0.014.
Values sent between devices are 32-bit elements; how exact they have to be, the bound alone decides.
A program may use at most 192 MiB of HBM per device.

v0:
```python
import functools
import math

import jax
import jax.numpy as jnp
import numpy as np
from jax import lax
from jax.experimental import pallas as pl
from jax.experimental.pallas import tpu as pltpu
from jax.sharding import PartitionSpec as P

HD = 128
FF_USED = 5461


deep_alpha = math.sqrt(48.0)
norm_eps = 1e-05
highest = lax.Precision.HIGHEST


def layer_norm(inputs, norm_gain, norm_bias):
    center = jnp.mean(inputs, axis=-1, keepdims=True)
    centered = inputs - center
    spread = jnp.mean(centered * centered, axis=-1, keepdims=True)
    return centered * lax.rsqrt(spread + norm_eps) * norm_gain + norm_bias


def rotary_tables(length, head_width):
    half_width = head_width // 2
    frequency = jnp.exp(
        jnp.arange(half_width, dtype=jnp.float32) * (-2.0 * math.log(10000.0) / head_width)
    )
    angles = jnp.arange(length, dtype=jnp.float32)[:, None] * frequency[None, :]
    return (jnp.cos(angles), jnp.sin(angles))


def rotate(inputs, cosine, sine):
    half_width = inputs.shape[-1] // 2
    first = inputs[..., :half_width]
    second = inputs[..., half_width:]
    cosine = cosine[:, None, :]
    sine = sine[:, None, :]
    return jnp.concatenate(
        [first * cosine - second * sine, second * cosine + first * sine], axis=-1
    )


def row_mask(row_begin, row_count, length, prefix):
    columns = jnp.arange(length, dtype=jnp.int32)
    row_index = row_begin + jnp.arange(row_count, dtype=jnp.int32)
    return (columns[None, :] < prefix) | (columns[None, :] <= row_index[:, None])


def block_scores(query_block, keys_rot, visible, score_scale):
    scores = (
        jnp.einsum("bhd,khd->hbk", query_block, keys_rot, preferred_element_type=jnp.float32)
        * score_scale
    )
    return jnp.where(visible[None, :, :], scores, -1e30)


def attention_forward(queries, keys_rot, values_in, prefix, row_block):
    length = queries.shape[0]
    score_scale = 1.0 / math.sqrt(HD)

    def one_block(row_begin):
        scores = block_scores(
            queries, keys_rot, row_mask(row_begin, row_block, length, prefix), score_scale
        )
        row_max = jnp.max(scores, axis=-1, keepdims=True)
        weights = jnp.exp(scores - row_max)
        total_weight = jnp.sum(weights, axis=-1, keepdims=True)
        probability = (weights / total_weight).astype(jnp.bfloat16)
        mixed_block = jnp.einsum(
            "hbk,khd->bhd", probability, values_in, preferred_element_type=jnp.float32
        )
        return (mixed_block, row_max + jnp.log(total_weight))

    starts = jnp.arange(length // row_block, dtype=jnp.int32) * row_block
    attended, log_total = lax.map(one_block, starts)
    return (attended.reshape(length, -1), log_total)


def attention_backward(queries, keys_rot, values_in, prefix, row_block, log_total, grad_mixed):
    length = queries.shape[0]
    score_scale = 1.0 / math.sqrt(HD)

    def one_block(carried, inputs):
        grad_keys, grad_values = carried
        row_begin, block_total = inputs
        scores = block_scores(
            queries, keys_rot, row_mask(row_begin, row_block, length, prefix), score_scale
        )
        probability = jnp.exp(scores - block_total)
        prob_low = probability.astype(jnp.bfloat16)
        grad_prob = jnp.einsum(
            "bhd,khd->hbk", grad_mixed, values_in, preferred_element_type=jnp.float32
        )
        centre = jnp.sum(grad_prob * probability, axis=-1, keepdims=True)
        grad_scores = (probability * (grad_prob - centre)).astype(jnp.bfloat16)
        grad_query = (
            jnp.einsum("hbk,khd->bhd", grad_scores, keys_rot, preferred_element_type=jnp.float32)
            * score_scale
        )
        grad_keys = (
            grad_keys
            + jnp.einsum("hbk,bhd->khd", grad_scores, queries, preferred_element_type=jnp.float32)
            * score_scale
        )
        grad_values = grad_values + jnp.einsum(
            "hbk,bhd->khd", prob_low, grad_mixed, preferred_element_type=jnp.float32
        )
        return ((grad_keys, grad_values), grad_query)

    starts = jnp.arange(length // row_block, dtype=jnp.int32) * row_block
    zeros_kv = jnp.zeros(keys_rot.shape, jnp.float32)
    (grad_keys, grad_values), grad_queries = lax.scan(
        one_block, (zeros_kv, zeros_kv), (starts, log_total)
    )
    return (grad_queries.reshape(queries.shape), grad_keys, grad_values)


def local_general(
    token_ids,
    prefix_lengths,
    cluster_ids,
    embedding,
    w_query,
    w_key,
    w_value,
    w_dense,
    w_gate,
    w_up,
    w_down,
    norm1_gain,
    norm1_bias,
    norm2_gain,
    norm2_bias,
    cotangent,
):
    length = token_ids.shape[0]
    vocab_rows = embedding.shape[0]
    row_block = min(512, length)
    local_heads = w_query.shape[1] // HD
    local_hidden = w_gate.shape[1]
    one_hot = (token_ids[:, None] == jnp.arange(vocab_rows, dtype=jnp.int32)[None, :]).astype(
        jnp.bfloat16
    )
    embedded_low = jnp.dot(one_hot, embedding, preferred_element_type=jnp.float32).astype(
        jnp.bfloat16
    )
    embedded = embedded_low.astype(jnp.float32)
    cosine, sine = rotary_tables(length, HD)
    prefix = prefix_lengths[0]
    own_cluster = cluster_ids[lax.axis_index("dp")]
    seq_weight = 1.0 / jnp.sum((cluster_ids == own_cluster).astype(jnp.float32))

    def project(weight_in):
        return jnp.dot(embedded_low, weight_in, preferred_element_type=jnp.float32).reshape(
            length, local_heads, HD
        )

    queries = rotate(project(w_query), cosine, sine).astype(jnp.bfloat16)
    keys_rot = rotate(project(w_key), cosine, sine).astype(jnp.bfloat16)
    values_in = project(w_value).astype(jnp.bfloat16)
    attended, log_total = attention_forward(queries, keys_rot, values_in, prefix, row_block)
    attended_low = attended.astype(jnp.bfloat16)
    branch = lax.psum(
        jnp.einsum("lh,dh->ld", attended_low, w_dense, preferred_element_type=jnp.float32), "mp"
    )
    residual_one = deep_alpha * embedded + branch
    hidden, norm_one_pull = jax.vjp(layer_norm, residual_one, norm1_gain, norm1_bias)
    hidden_low = hidden.astype(jnp.bfloat16)
    gate_proj = jnp.dot(hidden_low, w_gate, preferred_element_type=jnp.float32)
    up_proj = jnp.dot(hidden_low, w_up, preferred_element_type=jnp.float32)
    unit_index = lax.axis_index("mp") * local_hidden + jnp.arange(local_hidden, dtype=jnp.int32)
    used_mask = (unit_index < FF_USED).astype(jnp.float32)

    def gated_unit(gate_in, up_in):
        return jax.nn.gelu(gate_in, approximate=True) * up_in * used_mask

    activation, gated_pull = jax.vjp(gated_unit, gate_proj, up_proj)
    activation_low = activation.astype(jnp.bfloat16)
    branch_two = lax.psum(
        jnp.einsum("lf,df->ld", activation_low, w_down, preferred_element_type=jnp.float32), "mp"
    )
    residual_two = deep_alpha * hidden + branch_two
    final, norm_two_pull = jax.vjp(layer_norm, residual_two, norm2_gain, norm2_bias)
    grad_out = cotangent.astype(jnp.float32) * seq_weight
    grad_two, grad_gain_two, grad_bias_two = norm_two_pull(grad_out)
    grad_branch_two = grad_two.astype(jnp.bfloat16)
    grad_w_down = jnp.einsum(
        "ld,lf->df", grad_branch_two, activation_low, preferred_element_type=jnp.float32
    )
    grad_act = jnp.dot(grad_branch_two, w_down, preferred_element_type=jnp.float32)
    grad_gate, grad_up = gated_pull(grad_act)
    grad_gate_low = grad_gate.astype(jnp.bfloat16)
    grad_up_low = grad_up.astype(jnp.bfloat16)
    grad_w_gate = jnp.einsum(
        "ld,lf->df", hidden_low, grad_gate_low, preferred_element_type=jnp.float32
    )
    grad_w_up = jnp.einsum("ld,lf->df", hidden_low, grad_up_low, preferred_element_type=jnp.float32)
    hidden_part = jnp.einsum(
        "lf,df->ld", grad_gate_low, w_gate, preferred_element_type=jnp.float32
    ) + jnp.einsum("lf,df->ld", grad_up_low, w_up, preferred_element_type=jnp.float32)
    grad_hidden = deep_alpha * grad_two + lax.psum(hidden_part, "mp")
    feed_sums = (
        lax.psum_scatter(grad_w_gate, "dp", scatter_dimension=0, tiled=True),
        lax.psum_scatter(grad_w_up, "dp", scatter_dimension=0, tiled=True),
        lax.psum_scatter(grad_w_down, "dp", scatter_dimension=0, tiled=True),
        lax.psum_scatter(grad_gain_two, "dp", scatter_dimension=0, tiled=True),
        lax.psum_scatter(grad_bias_two, "dp", scatter_dimension=0, tiled=True),
    )
    grad_one, grad_gain_one, grad_bias_one = norm_one_pull(grad_hidden)
    grad_branch = grad_one.astype(jnp.bfloat16)
    grad_w_dense = jnp.einsum(
        "ld,lh->dh", grad_branch, attended_low, preferred_element_type=jnp.float32
    )
    grad_attended = jnp.dot(grad_branch, w_dense, preferred_element_type=jnp.float32).astype(
        jnp.bfloat16
    )
    grad_attended = grad_attended.reshape(length, local_heads, HD)
    grad_queries, grad_keys, grad_values = attention_backward(
        queries, keys_rot, values_in, prefix, row_block, log_total, grad_attended
    )
    grad_query_lin = rotate(grad_queries, cosine, -sine).astype(jnp.bfloat16).reshape(length, -1)
    grad_key_lin = rotate(grad_keys, cosine, -sine).astype(jnp.bfloat16).reshape(length, -1)
    grad_value_lin = grad_values.astype(jnp.bfloat16).reshape(length, -1)
    grad_w_query = jnp.einsum(
        "ld,lh->dh", embedded_low, grad_query_lin, preferred_element_type=jnp.float32
    )
    grad_w_key = jnp.einsum(
        "ld,lh->dh", embedded_low, grad_key_lin, preferred_element_type=jnp.float32
    )
    grad_w_value = jnp.einsum(
        "ld,lh->dh", embedded_low, grad_value_lin, preferred_element_type=jnp.float32
    )
    input_part = (
        jnp.einsum("lh,dh->ld", grad_query_lin, w_query, preferred_element_type=jnp.float32)
        + jnp.einsum("lh,dh->ld", grad_key_lin, w_key, preferred_element_type=jnp.float32)
        + jnp.einsum("lh,dh->ld", grad_value_lin, w_value, preferred_element_type=jnp.float32)
    )
    grad_embedded = deep_alpha * grad_one + lax.psum(input_part, "mp")
    grad_table = 0.1 * jnp.dot(one_hot.astype(jnp.float32).T, grad_embedded, precision=highest)
    attn_sums = (
        lax.psum_scatter(grad_table, "dp", scatter_dimension=0, tiled=True),
        lax.psum_scatter(grad_w_query, "dp", scatter_dimension=0, tiled=True),
        lax.psum_scatter(grad_w_key, "dp", scatter_dimension=0, tiled=True),
        lax.psum_scatter(grad_w_value, "dp", scatter_dimension=0, tiled=True),
        lax.psum_scatter(grad_w_dense, "dp", scatter_dimension=0, tiled=True),
        lax.psum_scatter(grad_gain_one, "dp", scatter_dimension=0, tiled=True),
        lax.psum_scatter(grad_bias_one, "dp", scatter_dimension=0, tiled=True),
    )
    summed = (
        attn_sums[0],
        attn_sums[1],
        attn_sums[2],
        attn_sums[3],
        attn_sums[4],
        feed_sums[0],
        feed_sums[1],
        feed_sums[2],
        attn_sums[5],
        attn_sums[6],
        feed_sums[3],
        feed_sums[4],
    )
    return (
        final.astype(jnp.bfloat16),
        summed[0],
        summed[1],
        summed[2],
        summed[3],
        summed[4],
        summed[5],
        summed[6],
        summed[7],
        summed[8],
        summed[9],
        summed[10],
        summed[11],
    )


LINE = 4
MESH = pl.DeviceIdType.MESH
CHUNKS = 4
AHEAD = 2
LOW = jnp.bfloat16
FULL = jnp.float32
TANH_SCALE = math.sqrt(2.0 / math.pi)


def dot(left, right):
    return jnp.dot(left, right, preferred_element_type=FULL)


def dot_nt(left, right):
    return lax.dot_general(left, right, (((1,), (1,)), ((), ())), preferred_element_type=FULL)


def dot_tn(left, right):
    return lax.dot_general(left, right, (((0,), (0,)), ((), ())), preferred_element_type=FULL)


def split_low(value):
    high = value.astype(LOW)
    return high, (value - high.astype(FULL)).astype(LOW)


def row_mean(value):
    return jnp.mean(value, axis=-1, keepdims=True)


def spread(size, body, tile=512):
    for start in range(0, size, tile):
        body(start, min(tile, size - start))


def tiles(size, body, tile=512):
    whole = size // tile
    lax.fori_loop(0, whole, lambda step, carried: (body(pl.multiple_of(step * tile, tile), tile), carried)[1], 0)
    if size % tile:
        body(whole * tile, size % tile)


def layer_kernel(
    length, width, local_hidden,
    prefix_ref, cluster_ref, ids_row, emb, cos_ref, sin_ref, norms, w_query_hbm, w_key_hbm, w_value_hbm, w_dense_hbm,
    w_gate_hbm, w_up_hbm, w_down_hbm, cot_hbm,
    block_out, out_table, out_query, out_key, out_value, out_dense, out_gate, out_up, out_down, out_norms,
    r_act, r_two, r_y, r_cols, r_att, xhat_park, grad_two_park, r_dny, r_rs, r_rsd, r_sums,
    parts, core_in, x_in, back_in, blocks, xbuf, gbuf, obuf, gate_up, grads_low, act_low, send_a, cols_own, cols_send,
    two_own, two_send, att_low, att_turned, heads, w_dense, one_hot, hot_turned, rstd_one, vectors, table_core, table_x,
    core_s, core_r, x_s, x_r, back_s, back_r, act_s, act_r, two_s, two_r, fwd_two_s, fwd_two_r, cols_s, cols_r, fwd_s,
    fwd_r, ys_s, ys_r, att_s, att_r, dny_s, dny_r, rs_s, rs_r, sums_s, sums_r, table_s, table_r, load_sem, weight_sem,
):
    dp, mp = lax.axis_index("dp"), lax.axis_index("mp")
    z, y = lax.div(dp, 2), lax.rem(dp, 2)
    x, core = lax.div(mp, 2), lax.rem(mp, 2)
    rows = length // CHUNKS
    heads_here = heads.shape[1]
    inner = heads_here * HD
    vocab = emb.shape[0]
    shift = (local_hidden + 15) // 16 * 16
    block = width // (2 * LINE)
    alpha = jnp.float32(deep_alpha)

    def at(z_to=None, y_to=None, x_to=None, core_to=None):
        z_to = z if z_to is None else z_to
        y_to = y if y_to is None else y_to
        x_to = x if x_to is None else x_to
        core_to = core if core_to is None else core_to
        return (2 * z_to + y_to, 2 * x_to + core_to)

    core_peer = at(core_to=1 - core)
    x_peer = at(x_to=1 - x)
    y_peer = at(y_to=1 - y)

    def remote(source, target, send, receive, device):
        return pltpu.make_async_remote_copy(
            src_ref=source, dst_ref=target, send_sem=send, recv_sem=receive,
            device_id=device, device_id_type=MESH,
        )

    def load_all(pairs):
        copies = [
            pltpu.make_async_copy(source, target, load_sem.at[place])
            for place, (source, target) in enumerate(pairs)
        ]
        for copy in copies:
            copy.start()
        return copies

    def moved(pairs):
        for copy in load_all(pairs):
            copy.wait()

    barrier = pltpu.get_barrier_semaphore()
    greeted = [core_peer, x_peer, y_peer] + [at(z_to=lax.rem(z + step, LINE)) for step in range(1, LINE)]
    for device in greeted:
        pl.semaphore_signal(barrier, inc=1, device_id=device, device_id_type=MESH)

    def chunk_rows(chunk):
        return pl.ds(pl.multiple_of(chunk * rows, rows), rows)

    def core_copy(turn, chunk):
        return remote(
            parts.at[chunk, 1 - core], core_in.at[chunk], core_s.at[turn, chunk], core_r.at[turn, chunk], core_peer
        )

    def x_copy(turn, chunk):
        return remote(
            parts.at[chunk, core], x_in.at[turn % 2, chunk], x_s.at[turn, chunk], x_r.at[turn, chunk], x_peer
        )

    def back_copy(turn, chunk):
        return remote(
            parts.at[chunk, core], back_in.at[chunk], back_s.at[turn, chunk], back_r.at[turn, chunk], core_peer
        )

    def put_part(chunk, start, size, value):
        lanes = pl.ds(pl.multiple_of(lax.rem(start, width // 2), size), size)
        parts[chunk, lax.div(start, width // 2), :, lanes] = value

    def send_part(turn, chunk):
        core_copy(turn, chunk).wait()
        parts[chunk, core] = parts[chunk, core] + core_in[chunk]
        x_copy(turn, chunk).start()

    def take_part(turn, chunk):
        x_copy(turn, chunk).wait()
        parts[chunk, core] = parts[chunk, core] + x_in[turn % 2, chunk]
        back = back_copy(turn, chunk)
        back.start()
        mine = parts[chunk, core]
        back.wait()
        other = back_in[chunk]
        return jnp.concatenate([jnp.where(core == 0, mine, other), jnp.where(core == 0, other, mine)], axis=1)

    def put_blocks(value):
        for place in range(2 * LINE):
            blocks[place] = value[:, place * block : (place + 1) * block]

    def chunk_lanes(chunk):
        return pl.ds(pl.multiple_of(chunk * rows, rows), rows)

    def half_lanes(side):
        return pl.ds(pl.multiple_of(side * block, block), block)

    def keep_columns(own, chunk):
        for place in range(LINE):
            own[place, chunk_rows(chunk), :] = blocks[2 * place + y].astype(LOW)
        for place in range(2):
            cols_send[place, chunk] = blocks[2 * (2 * core + place) + 1 - y]

    def cols_copy(kind, chunk):
        return remote(
            cols_send.at[:, chunk], r_cols.at[kind, pl.ds(2 * core, 2), chunk],
            cols_s.at[kind, chunk], cols_r.at[kind, chunk], y_peer,
        )

    def forward_copy(kind):
        view = r_cols.at[kind, pl.ds(2 * core, 2)]
        return remote(view, view, fwd_s.at[kind], fwd_r.at[kind], core_peer)

    def act_copy(way, hop, chunk):
        goal = jnp.clip(z + 1 - 2 * way, 0, LINE - 1)
        owner = z - hop if way == 0 else z + hop
        active = (owner >= 0) & (z < LINE - 1) if way == 0 else (owner < LINE) & (z > 0)
        owner = jnp.clip(owner, 0, LINE - 1)
        landed = r_act.at[owner, :, chunk_lanes(chunk)]
        source = send_a.at[lax.div(chunk, 2), :, half_chunk(chunk)] if hop == 0 else landed
        return active, remote(
            source, landed, act_s.at[way, hop, chunk], act_r.at[way, hop, chunk], at(z_to=goal)
        )

    def act_landed(way, hop):
        return z - 1 - hop >= 0 if way == 0 else z + 1 + hop < LINE

    def half_chunk(chunk):
        return pl.ds(pl.multiple_of(lax.rem(chunk, 2) * rows, rows), rows)

    def act_send(hop, chunk):
        for way in range(2):
            active, copy = act_copy(way, hop, chunk)
            pl.when(active)(copy.start)

    def act_take(hop, chunk):
        for way in range(2):
            _, copy = act_copy(way, hop, chunk)
            pl.when(act_landed(way, hop))(copy.wait_recv)

    def two_copy(step, chunk):
        goal = lax.rem(z + step, LINE)
        return remote(
            two_send.at[goal, chunk], r_two.at[z, core, chunk],
            two_s.at[step - 1, chunk], two_r.at[step - 1, chunk], at(z_to=goal),
        )

    def two_forward(step):
        view = r_two.at[lax.rem(z + step, LINE), core]
        return remote(view, view, fwd_two_s.at[step - 1], fwd_two_r.at[step - 1], core_peer)

    def pair_copy(which, chunk):
        return remote(
            gate_up.at[which, :, chunk_lanes(chunk)], r_y.at[which, :, chunk_lanes(chunk)],
            ys_s.at[which, chunk], ys_r.at[which, chunk], y_peer,
        )

    def rows_copy():
        return remote(gbuf, r_att, att_s, att_r, y_peer)

    def every_chunk(body):
        lax.fori_loop(0, CHUNKS, lambda chunk, carried: (body(chunk), carried)[1], 0)

    column = lax.broadcasted_iota(jnp.int32, (length, length), 1)
    row = lax.broadcasted_iota(jnp.int32, (length, length), 0)
    score_scale = 1.0 / math.sqrt(HD)

    def probabilities(queries, keys):
        visible = (column < prefix_ref[0]) | (column <= row)
        scores = jnp.where(visible, dot_nt(queries, keys) * score_scale, -1e30)
        weights = jnp.exp(scores - jnp.max(scores, axis=-1, keepdims=True))
        return weights / jnp.sum(weights, axis=-1, keepdims=True)

    def turn_by(value, sine):
        return value * cos_ref[...] + pltpu.roll(value, HD // 2, 1) * sine

    def head_lanes(place, offset=0):
        return pl.ds(pl.multiple_of(offset + place * HD, HD), HD)

    def first_scope(w_heads, tab):
        loads = [
            pltpu.make_async_copy(source, target, weight_sem.at[place])
            for place, (source, target) in enumerate(
                (
                    (w_query_hbm, w_heads.at[0]),
                    (w_key_hbm, w_heads.at[1]),
                    (w_value_hbm, w_heads.at[2]),
                    (w_dense_hbm, w_dense),
                )
            )
        ]
        for copy in loads:
            copy.start()
        named = lax.broadcasted_iota(jnp.int32, (vocab, length), 0) == ids_row[...]
        hot = jnp.where(named, 1.0, 0.0)
        hot_turned[...] = hot.astype(LOW)
        one_hot[...] = hot.T.astype(LOW)
        vectors[...] = jnp.zeros_like(vectors)
        for kind in range(3):
            loads[kind].wait()
            table = dot(emb[...], w_heads[kind])
            for place in range(heads_here):
                tab[kind * heads_here + place] = table[:, place * HD : (place + 1) * HD]

        def attend_head(place, carried):
            hot = one_hot[...]
            lin = []
            for kind in range(3):
                high, rest = split_low(tab[kind * heads_here + place])
                lin.append(dot(hot, high) + dot(hot, rest))
            queries = turn_by(lin[0], sin_ref[...]).astype(LOW)
            keys = turn_by(lin[1], sin_ref[...]).astype(LOW)
            values = lin[2].astype(LOW)
            heads[0, place], heads[1, place], heads[2, place] = queries, keys, values
            probability = probabilities(queries, keys).astype(LOW)
            mixed = dot(probability, values).astype(LOW)
            att_low[:, head_lanes(place)] = mixed
            turned = mixed.astype(FULL).T
            head_rows = pl.ds(pl.multiple_of(place * HD, HD), HD)
            att_turned[head_rows, :] = turned.astype(LOW)
            gbuf[head_rows, :] = turned
            return carried

        lax.fori_loop(0, heads_here, attend_head, 0)
        loads[3].wait()
        pl.semaphore_wait(barrier, len(greeted))

        def project(chunk):
            mixed = att_low[chunk_rows(chunk), :]

            def columns(start, size):
                put_part(chunk, start, size, dot_nt(mixed, w_dense[pl.ds(start, size), :]))

            tiles(width, columns)
            core_copy(0, chunk).start()
            pl.when((chunk > 0) & (chunk <= AHEAD))(lambda: send_part(0, chunk - 1))

        every_chunk(project)
        rows_copy().start()

    pl.run_scoped(first_scope, pltpu.VMEM((3, width, inner), LOW), pltpu.VMEM((3 * heads_here, vocab, HD), FULL))

    def middle_scope(w_gate, w_up, w_down, cotbuf):
        weight_copies = [
            pltpu.make_async_copy(source, target, weight_sem.at[place])
            for place, (source, target) in enumerate(((w_gate_hbm, w_gate), (w_up_hbm, w_up), (w_down_hbm, w_down)))
        ]
        for copy in weight_copies:
            copy.start()
        for copy in weight_copies:
            copy.wait()

        def feed_forward(chunk):
            branch = take_part(0, chunk)
            residual = alpha * dot(one_hot[chunk_rows(chunk), :], emb[...]) + branch
            centered = residual - row_mean(residual)
            rstd = lax.rsqrt(row_mean(centered * centered) + norm_eps)
            xhat = centered * rstd
            rstd_one[chunk] = rstd
            xbuf[...] = xhat
            park = pltpu.make_async_copy(xbuf, xhat_park.at[chunk], load_sem.at[0])
            park.start()
            hidden_low = (xhat * norms[0:1, :] + norms[1:2, :]).astype(LOW)
            put_blocks(hidden_low.astype(FULL))
            keep_columns(cols_own, chunk)
            cols_copy(0, chunk).start()

            def units_tile(start, size):
                cut = pl.ds(start, size)
                gate = dot_nt(w_gate[cut, :], hidden_low)
                up = dot_nt(w_up[cut, :], hidden_low)
                units = mp * local_hidden + start + lax.broadcasted_iota(jnp.int32, (size, rows), 0)
                used = jnp.where(units < FF_USED, 1.0, 0.0)
                square = gate * gate
                bend = jnp.tanh(TANH_SCALE * gate * (1.0 + 0.044715 * square))
                gelu = 0.5 * gate * (1.0 + bend) * used
                slope = 0.5 * (1.0 + bend) + 0.5 * gate * (1.0 - bend * bend) * (
                    TANH_SCALE * (1.0 + 3.0 * 0.044715 * square)
                )
                gate_up[0, cut, chunk_lanes(chunk)] = slope * up * used
                gate_up[1, cut, chunk_lanes(chunk)] = gelu
                active = (gelu * up).astype(LOW)
                act_low[cut, chunk_lanes(chunk)] = active
                send_a[lax.div(chunk, 2), cut, half_chunk(chunk)] = active.astype(FULL)

            tiles(local_hidden, units_tile)
            act_send(0, chunk)
            active = send_a[lax.div(chunk, 2), :, half_chunk(chunk)].T.astype(LOW)
            tiles(
                width, lambda start, size: put_part(chunk, start, size, dot(active, w_down[:, pl.ds(start, size)]))
            )
            core_copy(1, chunk).start()
            park.wait()
            send_part(1, chunk)
            pl.when(chunk + AHEAD < CHUNKS)(lambda: send_part(0, chunk + AHEAD))

        same = jnp.int32(0)
        for place in range(2 * LINE):
            same = same + jnp.where(cluster_ref[place] == cluster_ref[dp], 1, 0)
        weight_row = 1.0 / jnp.full((1, width), same, jnp.int32).astype(FULL)

        def feed_backward(chunk):
            loads = load_all(
                ((xhat_park.at[chunk], xbuf), (cot_hbm.at[chunk_rows(chunk)], cotbuf))
            )
            branch = take_part(1, chunk)
            for copy in loads:
                copy.wait()
            residual = alpha * (xbuf[...] * norms[0:1, :] + norms[1:2, :]) + branch
            centered = residual - row_mean(residual)
            rstd = lax.rsqrt(row_mean(centered * centered) + norm_eps)
            xhat = centered * rstd
            obuf[...] = (xhat * norms[2:3, :] + norms[3:4, :]).astype(LOW)
            grad_out = cotbuf[...].astype(FULL) * weight_row
            vectors[2:3, :] += jnp.sum(grad_out * xhat, axis=0, keepdims=True)
            vectors[3:4, :] += jnp.sum(grad_out, axis=0, keepdims=True)
            grad_x = grad_out * norms[2:3, :]
            grad_two = (grad_x - row_mean(grad_x) - xhat * row_mean(grad_x * xhat)) * rstd
            for place in range(width // inner):
                gbuf[place * rows : (place + 1) * rows, :] = grad_two[:, place * inner : (place + 1) * inner]
            stores = load_all(
                ((obuf, block_out.at[chunk_rows(chunk)]), (gbuf, grad_two_park.at[chunk]))
            )
            grad_low = grad_two.astype(LOW)
            put_blocks(grad_low.astype(FULL))
            for place in range(2):
                two_own[place, chunk_rows(chunk), :] = blocks[2 * z + place].astype(LOW)
            for place in range(LINE):
                two_send[place, chunk] = blocks[2 * place + core]
            for step in range(1, LINE):
                two_copy(step, chunk).start()

            def units_tile(start, size):
                cut = pl.ds(start, size)
                grad_act = dot_nt(w_down[cut, :], grad_low)
                for which in range(2):
                    low = (grad_act * gate_up[which, cut, chunk_lanes(chunk)]).astype(LOW)
                    grads_low[pl.ds(which * shift + start, size), chunk_lanes(chunk)] = low
                    gate_up[which, cut, chunk_lanes(chunk)] = low.astype(FULL)

            spread(local_hidden, units_tile)
            pair_copy(0, chunk).start()
            for copy in stores:
                copy.wait()

        def step(turn, carried):
            pl.when(turn < CHUNKS)(lambda: feed_forward(turn))
            pl.when(turn == 1)(lambda: rows_copy().wait())
            pl.when(turn > 0)(lambda: feed_backward(turn - 1))
            return carried

        lax.fori_loop(0, CHUNKS + 1, step, 0)

        def hidden_part(pair):
            both = pl.ds(pl.multiple_of(2 * rows * pair, 2 * rows), 2 * rows)
            grad_gate = gate_up[0, :, both].T.astype(LOW)
            grad_up = gate_up[1, :, both].T.astype(LOW)

            def columns(start, size):
                cut = pl.ds(start, size)
                value = dot(grad_gate, w_gate[:, cut]) + dot(grad_up, w_up[:, cut])
                put_part(2 * pair, start, size, value[:rows])
                put_part(2 * pair + 1, start, size, value[rows:])

            tiles(width, columns)
            for place in range(2):
                core_copy(2, 2 * pair + place).start()
            for place in range(2):
                send_part(2, 2 * pair + place)

        lax.fori_loop(0, CHUNKS // 2, lambda pair, carried: (hidden_part(pair), carried)[1], 0)

    pl.run_scoped(
        middle_scope,
        pltpu.VMEM((local_hidden, width), LOW),
        pltpu.VMEM((local_hidden, width), LOW),
        pltpu.VMEM((local_hidden, width), LOW),
        pltpu.VMEM((rows, width), LOW),
    )

    def last_scope(theirs, cols_theirs, two_theirs, att_theirs, send_b, stage, grad_att, grad_one_own, sums, sums_up, sums_down, sums_below, sums_above, late_own):
        def norm_backward(chunk):
            loads = load_all(((xhat_park.at[chunk], xbuf), (grad_two_park.at[chunk], gbuf)))
            branch = take_part(2, chunk)
            for copy in loads:
                copy.wait()
            grad_two = [gbuf[place * rows : (place + 1) * rows, :] for place in range(width // inner)]
            grad_hidden = alpha * jnp.concatenate(grad_two, axis=1) + branch
            xhat = xbuf[...]
            vectors[0:1, :] += jnp.sum(grad_hidden * xhat, axis=0, keepdims=True)
            vectors[1:2, :] += jnp.sum(grad_hidden, axis=0, keepdims=True)
            grad_x = grad_hidden * norms[0:1, :]
            grad_one = (grad_x - row_mean(grad_x) - xhat * row_mean(grad_x * xhat)) * rstd_one[chunk]
            put_blocks(grad_one)
            for place in range(2):
                grad_one_own[chunk_rows(chunk), place * block : (place + 1) * block] = blocks[2 * mp + place]
            grad_low = grad_one.astype(LOW)
            put_blocks(grad_low.astype(FULL))
            keep_columns(late_own, chunk)
            grad_mixed = dot(grad_low, w_dense[...]).astype(LOW)
            for place in range(heads_here):
                grad_att[place, chunk_rows(chunk), :] = grad_mixed[:, place * HD : (place + 1) * HD]

        def fetch_columns(kind):
            forward = forward_copy(kind)
            forward.start()
            forward.wait()
            for pair in range(2):
                moved(
                    [(r_cols.at[kind, 2 * pair + place], blocks.at[pl.ds(CHUNKS * place, CHUNKS)]) for place in range(2)]
                )
                for place in range(2):
                    for chunk in range(CHUNKS):
                        piece = blocks[CHUNKS * place + chunk].astype(LOW)
                        cols_theirs[kind, 2 * pair + place, chunk * rows : (chunk + 1) * rows, :] = piece

        def fetch_rows(source, target):
            size = source.shape[0]
            views = [stage.at[place, pl.ds(0, size)] for place in range(2)]
            moved([(source.at[:, pl.ds(block * place, block)], views[place]) for place in range(2)])
            for place in range(2):
                target[:, block * place : block * (place + 1)] = views[place][...].astype(LOW)

        def outer_product(target, kind, place, own, other):
            right, right_theirs = (cols_own, late_own)[kind][place], cols_theirs[kind, place]

            def rows_tile(start, size):
                cut = pl.ds(start, size)
                target[cut, :] = dot(own[cut, :], right) + dot(other[cut, :], right_theirs)

            tiles(target.shape[0], rows_tile)

        def down_products():
            for step in range(1, LINE):
                for chunk in range(CHUNKS):
                    two_copy(step, chunk).wait()
            for step in range(1, LINE):
                two_forward(step).start()
            for step in range(1, LINE):
                two_forward(step).wait()
            for chunk in range(CHUNKS):
                pl.when(at_end)(lambda: act_take(1, chunk))
                act_take(2, chunk)
            for step in range(LINE):
                owner = lax.rem(z + step, LINE)
                if step:
                    moved(
                        [
                            (r_two.at[owner, place], blocks.at[pl.ds(CHUNKS * place, CHUNKS)])
                            for place in range(2)
                        ]
                    )
                    for place in range(2):
                        for chunk in range(CHUNKS):
                            piece = blocks[CHUNKS * place + chunk].astype(LOW)
                            two_theirs[place, chunk * rows : (chunk + 1) * rows, :] = piece
                    fetch_rows(r_act.at[owner], theirs.at[0])
                left, right = (theirs.at[0], two_theirs) if step else (act_low, two_own)
                for place in range(2):
                    lanes = slice(place * block, (place + 1) * block)

                    def rows_tile(start, size):
                        cut = pl.ds(start, size)
                        product = dot(left[cut, :], right[place])
                        gate_up[0, cut, lanes] = gate_up[0, cut, lanes] + product if step else product

                    tiles(local_hidden, rows_tile)

        def down_copy():
            return remote(gate_up.at[0, :, half_lanes(1 - y)], r_dny, dny_s, dny_r, y_peer)

        def down_end():
            down_copy().wait()
            moved([(r_dny, stage.at[0])])
            stage[0] = stage[0] + gate_up[0, :, half_lanes(y)]
            moved([(stage.at[0], out_down)])
            for chunk in range(CHUNKS):
                for way in range(2):
                    for hop in range(1, LINE - 1):
                        active, copy = act_copy(way, hop, chunk)
                        pl.when(active)(copy.wait_send)

        def goes(slot, way):
            return z < slot if way == 0 else z > LINE - 1 - slot

        def inner_place(way):
            return z > 0 if way == 0 else z < LINE - 1

        def line_goal(way):
            return at(z_to=jnp.clip(z + 1 - 2 * way, 0, LINE - 1))

        def unit_terms(kind):
            return grads_low.at[pl.ds(pl.multiple_of(kind * shift, 16), local_hidden)], theirs.at[1 + kind]

        def count(way):
            return LINE - 1 - z if way == 0 else z

        def order(kind, slot, way):
            return kind * count(way) + slot - (LINE - count(way))

        def turn_of(number, way):
            many = jnp.maximum(count(way), 1)
            return lax.div(number, many) * (LINE - 1) + lax.rem(number, many) + LINE - 1 - count(way)

        def unit_copy(turn, way):
            kind, slot = lax.div(turn, LINE - 1), lax.rem(turn, LINE - 1)
            home = (send_a, send_b)[way].at[lax.rem(jnp.maximum(order(kind, slot + 1, way), 0), 2)]
            return remote(
                home, r_rs.at[kind, slot, way], rs_s.at[kind, slot, way], rs_r.at[kind, slot, way], line_goal(way)
            )

        def unit_sent(number, way):
            unit_copy(turn_of(jnp.maximum(number, 0), way), way).wait_send()

        def unit_slot(turn):
            kind, slot = lax.div(turn, LINE - 1), lax.rem(turn, LINE - 1) + 1
            own, other = unit_terms(kind)
            for way in range(2):

                @pl.when(goes(slot, way))
                def _():
                    number = order(kind, slot, way)
                    home = (send_a, send_b)[way].at[lax.rem(jnp.maximum(number, 0), 2)]
                    pl.when(number >= 2)(lambda: unit_sent(number - 2, way))
                    place = LINE - slot + z if way == 0 else slot - LINE + z
                    outer_product(home, 0, place, own, other)

                    @pl.when((slot > 1) & inner_place(way))
                    def _():
                        before = jnp.maximum(turn - 1, 0)
                        unit_copy(before, way).wait_recv()
                        landed = r_rs.at[lax.div(before, LINE - 1), lax.rem(before, LINE - 1), way]
                        moved([(landed, stage.at[way])])
                        home[...] = home[...] + stage[way]

                    unit_copy(turn, way).start()

        def unit_end(kind):
            own, other = unit_terms(kind)
            outer_product(stage.at[0], 0, z, own, other)
            for way in range(2):

                @pl.when(inner_place(way))
                def _():
                    unit_copy(kind * (LINE - 1) + LINE - 2, way).wait_recv()
                    moved([(r_rs.at[kind, LINE - 2, way], stage.at[1])])
                    stage[0] = stage[0] + stage[1]

            moved([(stage.at[0], (out_gate, out_up)[kind])])

        def late_home(slot, way):
            number = jnp.maximum(order(2, slot, way), 0)
            return (send_a, send_b)[way].at[lax.rem(number, 2), pl.ds(0, inner)]

        def late_copy(slot, way):
            return remote(
                late_home(slot, way), r_rsd.at[slot - 1, way], rs_s.at[2, slot - 1, way], rs_r.at[2, slot - 1, way],
                line_goal(way),
            )

        def late_slot(slot):
            for way in range(2):

                @pl.when(goes(slot, way))
                def _():
                    home = late_home(slot, way)
                    number = order(2, slot, way)
                    of_units = number - 2 < 2 * count(way)
                    pl.when(of_units)(lambda: unit_sent(number - 2, way))
                    if slot == LINE - 1:
                        pl.when(~of_units)(lambda: late_copy(slot - 2, way).wait_send())
                    place = LINE - slot + z if way == 0 else slot - LINE + z
                    outer_product(home, 1, place, att_turned, att_theirs)
                    if slot > 1:

                        @pl.when(inner_place(way))
                        def _():
                            late_copy(slot - 1, way).wait_recv()
                            arrived = stage.at[way, pl.ds(0, inner)]
                            moved([(r_rsd.at[slot - 2, way], arrived)])
                            home[...] = home[...] + arrived[...]

                    late_copy(slot, way).start()

        def last_sent(way):
            pl.when(goes(LINE - 1, way))(lambda: late_copy(LINE - 1, way).wait_send())
            pl.when(goes(LINE - 2, way))(lambda: late_copy(LINE - 2, way).wait_send())
            pl.when(count(way) == 1)(lambda: unit_sent(1, way))

        def late_end():
            total, arrived = stage.at[0, pl.ds(0, inner)], stage.at[1, pl.ds(0, inner)]
            outer_product(total, 1, z, att_turned, att_theirs)
            for way in range(2):

                @pl.when(inner_place(way))
                def _():
                    late_copy(LINE - 1, way).wait_recv()
                    moved([(r_rsd.at[LINE - 2, way], arrived)])
                    total[...] = total[...] + arrived[...]

            gbuf[0:block, :] = total[...].T
            moved([(gbuf.at[pl.ds(0, block)], out_dense)])
            for way in range(2):
                last_sent(way)

        def attention_backward(place, carried):
            hot_t = hot_turned[...]
            queries, keys, values = heads[0, place], heads[1, place], heads[2, place]
            grad_mixed = grad_att[place]
            probability = probabilities(queries, keys)
            grad_prob = dot_nt(grad_mixed, values)
            centre = jnp.sum(grad_prob * probability, axis=-1, keepdims=True)
            grad_scores = (probability * (grad_prob - centre)).astype(LOW)
            grad_queries = dot(grad_scores, keys) * score_scale
            grad_keys = dot_tn(grad_scores, queries) * score_scale
            grad_values = dot_tn(probability.astype(LOW), grad_mixed)
            sums[0, 0:vocab, head_lanes(place)] = dot(hot_t, turn_by(grad_queries, -sin_ref[...]).astype(LOW))
            sums[0, 0:vocab, head_lanes(place, inner)] = dot(hot_t, turn_by(grad_keys, -sin_ref[...]).astype(LOW))
            sums[1, 0:vocab, head_lanes(place)] = dot(hot_t, grad_values.astype(LOW))
            return carried

        def small_sums():
            lax.fori_loop(0, heads_here, attention_backward, 0)
            hot_t = hot_turned[...]
            high, rest = split_low(grad_one_own[...])
            sums[1, 0:vocab, heads_here * HD :] = dot(hot_t, high) + dot(hot_t, rest)
            for side in range(2):
                sums[side, vocab:, :] = vectors[:, side * (width // 2) : (side + 1) * (width // 2)]
            sums_pair().start()

        def sums_pair():
            return remote(sums.at[1 - y], r_sums.at[0], sums_s.at[0], sums_r.at[0], y_peer)

        def sums_line(way):
            source = (sums_up, sums_down)[way]
            goal = jnp.clip(z + 1 - 2 * way, 0, LINE - 1)
            return remote(source, r_sums.at[1 + way], sums_s.at[1 + way], sums_r.at[1 + way], at(z_to=goal))

        def sums_back():
            return remote(sums.at[y], r_sums.at[3], sums_s.at[3], sums_r.at[3], y_peer)

        def sums_first():
            sums_pair().wait()
            moved([(r_sums.at[0], sums_below)])
            sums[y] = sums[y] + sums_below[...]

            @pl.when(z == 0)
            def _():
                sums_up[...] = sums[y]
                sums_line(0).start()

            @pl.when(z == LINE - 1)
            def _():
                sums_down[...] = sums[y]
                sums_line(1).start()

        def sums_up_step():
            sums_line(0).wait_recv()
            moved([(r_sums.at[1], sums_below)])
            sums_up[...] = sums[y] + sums_below[...]
            sums_line(0).start()

        def sums_down_step():
            sums_line(1).wait_recv()
            moved([(r_sums.at[2], sums_above)])
            sums_down[...] = sums[y] + sums_above[...]
            sums_line(1).start()

        def sums_near():
            pl.when(z == 1)(sums_up_step)
            pl.when(z == LINE - 2)(sums_down_step)

        def sums_far():
            pl.when(z == LINE - 2)(sums_up_step)
            pl.when(z == 1)(sums_down_step)

        def sums_middle():
            @pl.when(z == LINE - 1)
            def _():
                sums_line(0).wait_recv()
                moved([(r_sums.at[1], sums_below)])

            @pl.when(z == 0)
            def _():
                sums_line(1).wait_recv()
                moved([(r_sums.at[2], sums_above)])

            @pl.when(z > 0)
            def _():
                sums[y] = sums[y] + sums_below[...]

            @pl.when(z < LINE - 1)
            def _():
                sums[y] = sums[y] + sums_above[...]

            sums_back().start()

        def sums_end():
            sums_back().wait()
            pl.when(z < LINE - 1)(sums_line(0).wait_send)
            pl.when(z > 0)(sums_line(1).wait_send)
            moved([(r_sums.at[3], sums.at[1 - y])])
            lanes = pl.ds(pl.multiple_of(lax.rem(dp, LINE) * block, block), block)
            moved([(sums.at[lax.div(dp, LINE), pl.ds(vocab, 8), lanes], out_norms)])

        def by_token(kind, rows_of):
            side, start = ((0, 0), (0, inner), (1, 0), (1, inner))[kind]
            return sums[side, rows_of, start : start + inner]

        def head_gradients():
            own_columns = emb[:, pl.ds(pl.multiple_of(dp * block, block), block)]
            for kind, result in enumerate((out_query, out_key, out_value)):
                high, rest = split_low(by_token(kind, slice(0, vocab)))
                gbuf[0:block, :] = dot_tn(own_columns, high) + dot_tn(own_columns, rest)
                moved([(gbuf.at[pl.ds(0, block)], result)])

        table_rows = vocab // (2 * LINE)
        table_own = pl.ds(pl.multiple_of(dp * table_rows, table_rows), table_rows)

        def table_part():
            for kind, weight in enumerate((w_query_hbm, w_key_hbm, w_value_hbm)):
                moved([(weight, w_dense)])
                pieces = jnp.concatenate(split_low(by_token(kind, table_own)), axis=0)

                def columns(start, size):
                    cut = pl.ds(start, size)
                    both = dot_nt(pieces, w_dense[cut, :])
                    both = both[:table_rows] + both[table_rows:]
                    xbuf[0:table_rows, cut] = both if kind == 0 else xbuf[0:table_rows, cut] + both

                tiles(width, columns)
            quarter = pl.ds(pl.multiple_of(mp * inner, inner), inner)
            xbuf[0:table_rows, quarter] = xbuf[0:table_rows, quarter] + alpha * by_token(3, table_own)
            table_copy(0).start()

        def table_middle():
            table_copy(0).wait()
            xbuf[table_rows : 2 * table_rows, :] = xbuf[0:table_rows, :] + table_core[...]
            table_copy(1).start()

        def table_end():
            table_copy(1).wait()
            xbuf[0:table_rows, :] = 0.1 * (xbuf[table_rows : 2 * table_rows, :] + table_x[...])
            moved([(xbuf.at[pl.ds(0, table_rows)], out_table)])

        def table_copy(turn):
            target, device = ((table_core, core_peer), (table_x, x_peer))[turn]
            return remote(xbuf.at[pl.ds(turn * table_rows, table_rows)], target, table_s.at[turn], table_r.at[turn], device)

        def act_pass():
            for chunk in range(CHUNKS):
                act_take(1, chunk)
                act_send(2, chunk)

        def down_all():
            down_products()
            down_copy().start()

        at_end = (z == 0) | (z == LINE - 1)

        for chunk in range(CHUNKS):
            cols_copy(0, chunk).wait()
        fetch_columns(0)
        for chunk in range(CHUNKS):
            pair_copy(0, chunk).wait()
        pair_copy(1, 0).start()
        pair_copy(1, 1).start()
        fetch_rows(r_y.at[0], theirs.at[1])
        for chunk in range(CHUNKS):
            for way in range(2):
                active, copy = act_copy(way, 0, chunk)
                pl.when(active)(copy.wait_send)
        def one_turn(turn, carried):
            unit_slot(turn)

            @pl.when(turn == 0)
            def _():
                for chunk in range(CHUNKS):
                    act_take(0, chunk)
                    act_send(1, chunk)

            @pl.when(turn == 1)
            def _():
                every_chunk(norm_backward)
                small_sums()
                pl.when(~at_end)(act_pass)
                sums_first()
                pair_copy(1, 2).start()
                pair_copy(1, 3).start()
                for chunk in range(CHUNKS):
                    cols_copy(1, chunk).start()

            @pl.when(turn == 2)
            def _():
                for chunk in range(CHUNKS):
                    pair_copy(1, chunk).wait()
                fetch_rows(r_y.at[1], theirs.at[2])

            pl.when(turn == 3)(sums_near)
            pl.when((turn == 3) & ~at_end | (turn == 5) & at_end)(down_all)
            pl.when(turn == 4)(sums_far)
            return carried

        lax.fori_loop(0, 2 * (LINE - 1), one_turn, 0)
        unit_end(0)
        for chunk in range(CHUNKS):
            cols_copy(1, chunk).wait()
        fetch_columns(1)
        fetch_rows(r_att, att_theirs)
        late_slot(1)
        sums_middle()
        sums_end()
        head_gradients()
        table_part()
        late_slot(2)
        table_middle()
        unit_end(1)
        late_slot(3)
        table_end()
        down_end()
        late_end()

    pl.run_scoped(
        last_scope,
        pltpu.VMEM((3, local_hidden, length), LOW),
        pltpu.VMEM((2, LINE, length, block), LOW),
        pltpu.VMEM((2, length, block), LOW),
        pltpu.VMEM((inner, length), LOW),
        pltpu.VMEM((2, local_hidden, block), FULL),
        pltpu.VMEM((2, local_hidden, block), FULL),
        pltpu.VMEM((heads_here, length, HD), LOW),
        pltpu.VMEM((length, 2 * block), FULL),
        pltpu.VMEM((2,) + r_sums.shape[1:], FULL),
        pltpu.VMEM(r_sums.shape[1:], FULL),
        pltpu.VMEM(r_sums.shape[1:], FULL),
        pltpu.VMEM(r_sums.shape[1:], FULL),
        pltpu.VMEM(r_sums.shape[1:], FULL),
        pltpu.VMEM(cols_own.shape, LOW),
    )


def local_fast(
    token_ids,
    prefix_lengths,
    cluster_ids,
    embedding,
    w_query,
    w_key,
    w_value,
    w_dense,
    w_gate,
    w_up,
    w_down,
    norm1_gain,
    norm1_bias,
    norm2_gain,
    norm2_bias,
    cotangent,
):
    length = token_ids.shape[0]
    vocab, width = embedding.shape
    inner = w_query.shape[1]
    heads_here = inner // HD
    local_hidden = w_gate.shape[1]
    rows = length // CHUNKS
    block = width // (2 * LINE)
    shift = (local_hidden + 15) // 16 * 16
    frequency = 10000.0 ** (np.arange(HD // 2) * (-2.0 / HD))
    angles = np.arange(length)[:, None] * frequency[None, :]
    cosine = np.concatenate([np.cos(angles)] * 2, axis=1).astype(np.float32)
    sine = np.concatenate([-np.sin(angles), np.sin(angles)], axis=1).astype(np.float32)
    norms = jnp.stack([norm1_gain, norm1_bias, norm2_gain, norm2_bias])

    hbm = pl.BlockSpec(memory_space=pl.ANY)
    vmem = pl.BlockSpec(memory_space=pltpu.VMEM)
    smem = pl.BlockSpec(memory_space=pltpu.SMEM)
    sums_rows = vocab + 8
    table_rows = vocab // (2 * LINE)
    shapes = [
        ((length, width), LOW),
        ((table_rows, width), FULL),
        ((block, inner), FULL),
        ((block, inner), FULL),
        ((block, inner), FULL),
        ((block, inner), FULL),
        ((local_hidden, block), FULL),
        ((local_hidden, block), FULL),
        ((local_hidden, block), FULL),
        ((8, block), FULL),
        ((LINE, local_hidden, length), FULL),
        ((LINE, 2, CHUNKS, rows, block), FULL),
        ((2, local_hidden, length), FULL),
        ((2, LINE, CHUNKS, rows, block), FULL),
        ((inner, length), FULL),
        ((CHUNKS, rows, width), FULL),
        ((CHUNKS, length, inner), FULL),
        ((local_hidden, block), FULL),
        ((2, LINE - 1, 2, local_hidden, block), FULL),
        ((LINE - 1, 2, inner, block), FULL),
        ((4, sums_rows, width // 2), FULL),
    ]
    scratch = [
        ((CHUNKS, 2, rows, width // 2), FULL),
        ((CHUNKS, rows, width // 2), FULL),
        ((2, CHUNKS, rows, width // 2), FULL),
        ((CHUNKS, rows, width // 2), FULL),
        ((2 * LINE, rows, block), FULL),
        ((rows, width), FULL),
        ((length, inner), FULL),
        ((rows, width), LOW),
        ((2, local_hidden, length), FULL),
        ((2 * shift, length), LOW),
        ((local_hidden, length), LOW),
        ((2, local_hidden, block), FULL),
        ((LINE, length, block), LOW),
        ((2, CHUNKS, rows, block), FULL),
        ((2, length, block), LOW),
        ((LINE, CHUNKS, rows, block), FULL),
        ((length, inner), LOW),
        ((inner, length), LOW),
        ((3, heads_here, length, HD), LOW),
        ((width, inner), LOW),
        ((length, vocab), LOW),
        ((vocab, length), LOW),
        ((CHUNKS, rows, 1), FULL),
        ((8, width), FULL),
        ((table_rows, width), FULL),
        ((table_rows, width), FULL),
    ]
    dma = pltpu.SemaphoreType.DMA
    each = (3, CHUNKS)
    semaphores = [
        each, each, each, each, each, each, (2, LINE - 1, CHUNKS), (2, LINE - 1, CHUNKS), each, each, (3,), (3,),
        (2, CHUNKS), (2, CHUNKS), (2,), (2,), (2, CHUNKS), (2, CHUNKS), None, None, None, None,
        (3, LINE - 1, 2), (3, LINE - 1, 2), (4,), (4,), (2,), (2,), (4,), (4,),
    ]
    results = pl.pallas_call(
        functools.partial(layer_kernel, length, width, local_hidden),
        out_shape=[jax.ShapeDtypeStruct(shape, dtype) for shape, dtype in shapes],
        in_specs=[smem] * 2 + [vmem] * 5 + [hbm] * 8,
        out_specs=[hbm] * len(shapes),
        scratch_shapes=[pltpu.VMEM(shape, dtype) for shape, dtype in scratch]
        + [dma if shape is None else dma(shape) for shape in semaphores],
        compiler_params=pltpu.CompilerParams(
            collective_id=0, has_side_effects=True, vmem_limit_bytes=62 * 2**20
        ),
    )(
        prefix_lengths,
        cluster_ids,
        token_ids.reshape(1, length),
        embedding,
        cosine,
        sine,
        norms,
        w_query,
        w_key,
        w_value,
        w_dense,
        w_gate.T,
        w_up.T,
        w_down.T,
        cotangent,
    )
    block_out, table, out_query, out_key, out_value, out_dense, out_gate, out_up, out_down, out_norms = results[:10]
    return (
        block_out,
        table,
        out_query,
        out_key,
        out_value,
        out_dense,
        out_gate.T,
        out_up.T,
        out_down.T,
        out_norms[0],
        out_norms[1],
        out_norms[2],
        out_norms[3],
    )


def solution(mesh):
    fast = mesh.shape["dp"] == 2 * LINE and mesh.shape["mp"] == 4
    return jax.shard_map(
        local_fast if fast else local_general,
        mesh=mesh,
        in_specs=(
            P("dp"),
            P("dp"),
            P(),
            P(),
            P(None, "mp"),
            P(None, "mp"),
            P(None, "mp"),
            P(None, "mp"),
            P(None, "mp"),
            P(None, "mp"),
            P(None, "mp"),
            P(),
            P(),
            P(),
            P(),
            P("dp", None),
        ),
        out_specs=(
            P("dp", None),
            P("dp", None),
            P("dp", "mp"),
            P("dp", "mp"),
            P("dp", "mp"),
            P("dp", "mp"),
            P("dp", "mp"),
            P("dp", "mp"),
            P("dp", "mp"),
            P("dp"),
            P("dp"),
            P("dp"),
            P("dp"),
        ),
        check_vma=False,
    )
```

profile of v0, /device:TPU:30, one launch (start us, length us, event | category | flops | bytes accessed | tf_op | source)
XLA Modules:
  0.0 395.3 jit_solution(16660906702572837797)
XLA Ops:
  1.3 1.4 pad_maximum_fusion.norms
  2.7 380.0 %shard_map.273 = (bf16[512,2048]{1,0:T(8,128)(2,1)}, f32[16,2048]{1,0:T(8,128)}, f32[256,512]{1,0:T(8,128)}, f32[256,512]{1,0:T(8,128)}, f32[256,512]{1,0:T(8,12...) custom-call(s32[1]{0:T(128)S(6)} %copy.40.prefix_ref, ...), custom_call_target="tpu_custom_call" | custom-call | tf_op jit(solution)/shard_map/pallas_call | solution.py:1270
  382.7 1.4 fusion
  384.1 0.0 copy-start.7
  384.1 0.0 copy-start.6
  384.1 0.0 copy-start.5
  384.2 3.3 copy.41
  387.4 0.0 copy-done.7
  387.4 0.0 copy-start.4
  387.4 0.0 copy-start.3
  387.4 0.7 copy.42
  388.1 0.0 copy-done.6
  388.1 0.0 copy-start.2
  388.1 0.8 copy.43
  388.9 0.0 copy-done.5
  388.9 0.8 copy.44
  389.7 0.0 copy-done.4
  389.7 0.8 copy.45
  390.5 0.0 copy-done.3
  390.5 0.0 copy-start.1
  390.5 0.8 copy.46
  391.3 0.0 copy-done.2
  391.3 1.1 copy.47
  392.3 0.0 copy-done.1
  392.4 0.0 copy-start
  392.4 1.1 copy.48
  393.4 0.8 copy-done
  394.2 1.1 copy.49
Async XLA Ops:
  384.1 3.3 copy-start.7
  384.1 3.9 copy-start.6
  384.1 4.7 %copy-start.5 = (f32[256,512]{1,0:T(8,128)S(1)}, f32[256,512]{1,0:T(8,128)}, u32[]{:S(2)}) copy-start(f32[256,512]{1,0:T(8,128)} %get-tuple-element.53) | copy-start | bytes 1572868
  387.4 2.3 copy-start.4
  387.4 3.1 copy-start.3
  388.1 3.2 copy-start.2
  390.5 1.9 copy-start.1
  392.4 1.9 copy-start
where the time goes:
time: 400 us; the launch traced here: 395 us
  Pallas kernels  380 us (95%)
  local copies, waits for them, and re-layouts  12.6 us (3%)
    pallas_call x1, Pallas kernels, local_fast(): pl.pallas_call(functools.partial(layer_kernel, length, width, local_hidde...  380 us
    unnamed x25, local copies, waits for them, and re-layouts  11.1 us

commit v1 on v0

--- a/solution.py
+++ b/solution.py
@@ -326,12 +326,12 @@
 
 def layer_kernel(
     length, width, local_hidden,
-    prefix_ref, cluster_ref, ids_row, emb, cos_ref, sin_ref, norms, w_query_hbm, w_key_hbm, w_value_hbm, w_dense_hbm,
+    prefix_ref, cluster_ref, ids_row, emb, cos_ref, sin_ref, gain_one, bias_one, gain_two, bias_two, w_query_hbm, w_key_hbm, w_value_hbm, w_dense_hbm,
     w_gate_hbm, w_up_hbm, w_down_hbm, cot_hbm,
     block_out, out_table, out_query, out_key, out_value, out_dense, out_gate, out_up, out_down, out_norms,
     r_act, r_two, r_y, r_cols, r_att, xhat_park, grad_two_park, r_dny, r_rs, r_rsd, r_sums,
     parts, core_in, x_in, back_in, blocks, xbuf, gbuf, obuf, gate_up, grads_low, act_low, send_a, cols_own, cols_send,
-    two_own, two_send, att_low, att_turned, heads, w_dense, one_hot, hot_turned, rstd_one, vectors, table_core, table_x,
+    hidden_theirs, two_own, two_send, att_low, att_turned, heads, w_dense, one_hot, hot_turned, rstd_one, vectors, table_core, table_x,
     core_s, core_r, x_s, x_r, back_s, back_r, act_s, act_r, two_s, two_r, fwd_two_s, fwd_two_r, cols_s, cols_r, fwd_s,
     fwd_r, ys_s, ys_r, att_s, att_r, dny_s, dny_r, rs_s, rs_r, sums_s, sums_r, table_s, table_r, load_sem, weight_sem,
 ):
@@ -343,6 +343,8 @@
     inner = heads_here * HD
     vocab = emb.shape[0]
     shift = (local_hidden + 15) // 16 * 16
+    near = (local_hidden // 2 + 15) // 16 * 16
+    spans = ((0, near), (near, local_hidden - near))
     block = width // (2 * LINE)
     alpha = jnp.float32(deep_alpha)
 
@@ -400,8 +402,8 @@
         )
 
     def put_part(chunk, start, size, value):
-        lanes = pl.ds(pl.multiple_of(lax.rem(start, width // 2), size), size)
-        parts[chunk, lax.div(start, width // 2), :, lanes] = value
+        side, first = lax.div(start, width // 2), lax.rem(start, width // 2)
+        parts[chunk, side, :, pl.ds(pl.multiple_of(first, size), size)] = value
 
     def send_part(turn, chunk):
         core_copy(turn, chunk).wait()
@@ -482,14 +484,32 @@
         view = r_two.at[lax.rem(z + step, LINE), core]
         return remote(view, view, fwd_two_s.at[step - 1], fwd_two_r.at[step - 1], core_peer)
 
-    def pair_copy(which, chunk):
+    def pair_copy(which, chunk, part):
+        units = pl.ds(*spans[part])
         return remote(
-            gate_up.at[which, :, chunk_lanes(chunk)], r_y.at[which, :, chunk_lanes(chunk)],
-            ys_s.at[which, chunk], ys_r.at[which, chunk], y_peer,
-        )
+            gate_up.at[which, units, chunk_lanes(chunk)], r_y.at[which, units, chunk_lanes(chunk)],
+            ys_s.at[which, chunk, part], ys_r.at[which, chunk, part], y_peer,
+        )
+
+    def pair_send(which, chunk):
+        for part in range(2):
+            pair_copy(which, chunk, part).start()
 
     def rows_copy():
         return remote(gbuf, r_att, att_s, att_r, y_peer)
+
+    def fetch_columns(kind, target):
+        forward = forward_copy(kind)
+        forward.start()
+        forward.wait()
+        for pair in range(2):
+            moved(
+                [(r_cols.at[kind, 2 * pair + place], blocks.at[pl.ds(CHUNKS * place, CHUNKS)]) for place in range(2)]
+            )
+            for place in range(2):
+                for chunk in range(CHUNKS):
+                    piece = blocks[CHUNKS * place + chunk].astype(LOW)
+                    target[2 * pair + place, chunk * rows : (chunk + 1) * rows, :] = piece
 
     def every_chunk(body):
         lax.fori_loop(0, CHUNKS, lambda chunk, carried: (body(chunk), carried)[1], 0)
@@ -564,7 +584,7 @@
             def columns(start, size):
                 put_part(chunk, start, size, dot_nt(mixed, w_dense[pl.ds(start, size), :]))
 
-            tiles(width, columns)
+            spread(width, columns, 256)
             core_copy(0, chunk).start()
             pl.when((chunk > 0) & (chunk <= AHEAD))(lambda: send_part(0, chunk - 1))
 
@@ -593,7 +613,7 @@
             xbuf[...] = xhat
             park = pltpu.make_async_copy(xbuf, xhat_park.at[chunk], load_sem.at[0])
             park.start()
-            hidden_low = (xhat * norms[0:1, :] + norms[1:2, :]).astype(LOW)
+            hidden_low = (xhat * gain_one[...] + bias_one[...]).astype(LOW)
             put_blocks(hidden_low.astype(FULL))
             keep_columns(cols_own, chunk)
             cols_copy(0, chunk).start()
@@ -639,15 +659,15 @@
             branch = take_part(1, chunk)
             for copy in loads:
                 copy.wait()
-            residual = alpha * (xbuf[...] * norms[0:1, :] + norms[1:2, :]) + branch
+            residual = alpha * (xbuf[...] * gain_one[...] + bias_one[...]) + branch
             centered = residual - row_mean(residual)
             rstd = lax.rsqrt(row_mean(centered * centered) + norm_eps)
             xhat = centered * rstd
-            obuf[...] = (xhat * norms[2:3, :] + norms[3:4, :]).astype(LOW)
+            obuf[...] = (xhat * gain_two[...] + bias_two[...]).astype(LOW)
             grad_out = cotbuf[...].astype(FULL) * weight_row
             vectors[2:3, :] += jnp.sum(grad_out * xhat, axis=0, keepdims=True)
             vectors[3:4, :] += jnp.sum(grad_out, axis=0, keepdims=True)
-            grad_x = grad_out * norms[2:3, :]
+            grad_x = grad_out * gain_two[...]
             grad_two = (grad_x - row_mean(grad_x) - xhat * row_mean(grad_x * xhat)) * rstd
             for place in range(width // inner):
                 gbuf[place * rows : (place + 1) * rows, :] = grad_two[:, place * inner : (place + 1) * inner]
@@ -672,17 +692,9 @@
                     gate_up[which, cut, chunk_lanes(chunk)] = low.astype(FULL)
 
             spread(local_hidden, units_tile)
-            pair_copy(0, chunk).start()
+            pair_send(0, chunk)
             for copy in stores:
                 copy.wait()
-
-        def step(turn, carried):
-            pl.when(turn < CHUNKS)(lambda: feed_forward(turn))
-            pl.when(turn == 1)(lambda: rows_copy().wait())
-            pl.when(turn > 0)(lambda: feed_backward(turn - 1))
-            return carried
-
-        lax.fori_loop(0, CHUNKS + 1, step, 0)
 
         def hidden_part(pair):
             both = pl.ds(pl.multiple_of(2 * rows * pair, 2 * rows), 2 * rows)
@@ -698,10 +710,24 @@
             tiles(width, columns)
             for place in range(2):
                 core_copy(2, 2 * pair + place).start()
-            for place in range(2):
-                send_part(2, 2 * pair + place)
-
-        lax.fori_loop(0, CHUNKS // 2, lambda pair, carried: (hidden_part(pair), carried)[1], 0)
+
+        def take_hidden():
+            for chunk in range(CHUNKS):
+                cols_copy(0, chunk).wait()
+            fetch_columns(0, hidden_theirs)
+
+        def step(turn, carried):
+            pl.when(turn == CHUNKS - 1)(lambda: hidden_part(0))
+            pl.when(turn == CHUNKS)(take_hidden)
+            pl.when(turn < CHUNKS)(lambda: feed_forward(turn))
+            pl.when(turn == 1)(lambda: rows_copy().wait())
+            pl.when(turn > 0)(lambda: feed_backward(turn - 1))
+            return carried
+
+        lax.fori_loop(0, CHUNKS + 1, step, 0)
+
+        hidden_part(1)
+        every_chunk(lambda chunk: send_part(2, chunk))
 
     pl.run_scoped(
         middle_scope,
@@ -711,7 +737,7 @@
         pltpu.VMEM((rows, width), LOW),
     )
 
-    def last_scope(theirs, cols_theirs, two_theirs, att_theirs, send_b, stage, grad_att, grad_one_own, sums, sums_up, sums_down, sums_below, sums_above, late_own):
+    def last_scope(theirs, late_theirs, two_theirs, att_theirs, send_b, stage, grad_att, grad_one_own, sums, sums_up, sums_down, sums_below, sums_above, late_own):
         def norm_backward(chunk):
             loads = load_all(((xhat_park.at[chunk], xbuf), (grad_two_park.at[chunk], gbuf)))
             branch = take_part(2, chunk)
@@ -722,7 +748,7 @@
             xhat = xbuf[...]
             vectors[0:1, :] += jnp.sum(grad_hidden * xhat, axis=0, keepdims=True)
             vectors[1:2, :] += jnp.sum(grad_hidden, axis=0, keepdims=True)
-            grad_x = grad_hidden * norms[0:1, :]
+            grad_x = grad_hidden * gain_one[...]
             grad_one = (grad_x - row_mean(grad_x) - xhat * row_mean(grad_x * xhat)) * rstd_one[chunk]
             put_blocks(grad_one)
             for place in range(2):
@@ -734,18 +760,16 @@
             for place in range(heads_here):
                 grad_att[place, chunk_rows(chunk), :] = grad_mixed[:, place * HD : (place + 1) * HD]
 
-        def fetch_columns(kind):
-            forward = forward_copy(kind)
-            forward.start()
-            forward.wait()
-            for pair in range(2):
-                moved(
-                    [(r_cols.at[kind, 2 * pair + place], blocks.at[pl.ds(CHUNKS * place, CHUNKS)]) for place in range(2)]
-                )
-                for place in range(2):
-                    for chunk in range(CHUNKS):
-                        piece = blocks[CHUNKS * place + chunk].astype(LOW)
-                        cols_theirs[kind, 2 * pair + place, chunk * rows : (chunk + 1) * rows, :] = piece
+        def fetch_units(which, part):
+            start, size = spans[part]
+            for chunk in range(CHUNKS):
+                pair_copy(which, chunk, part).wait()
+            views = [stage.at[side, pl.ds(start, size)] for side in range(2)]
+            moved(
+                [(r_y.at[which, pl.ds(start, size), pl.ds(block * side, block)], views[side]) for side in range(2)]
+            )
+            for side in range(2):
+                theirs[1 + which, start : start + size, block * side : block * (side + 1)] = views[side][...].astype(LOW)
 
         def fetch_rows(source, target):
             size = source.shape[0]
@@ -755,7 +779,7 @@
                 target[:, block * place : block * (place + 1)] = views[place][...].astype(LOW)
 
         def outer_product(target, kind, place, own, other):
-            right, right_theirs = (cols_own, late_own)[kind][place], cols_theirs[kind, place]
+            right, right_theirs = (cols_own, late_own)[kind][place], (hidden_theirs, late_theirs)[kind][place]
 
             def rows_tile(start, size):
                 cut = pl.ds(start, size)
@@ -835,38 +859,44 @@
             many = jnp.maximum(count(way), 1)
             return lax.div(number, many) * (LINE - 1) + lax.rem(number, many) + LINE - 1 - count(way)
 
-        def unit_copy(turn, way):
+        def unit_copy(turn, way, part):
             kind, slot = lax.div(turn, LINE - 1), lax.rem(turn, LINE - 1)
-            home = (send_a, send_b)[way].at[lax.rem(jnp.maximum(order(kind, slot + 1, way), 0), 2)]
+            units = pl.ds(*spans[part])
+            home = (send_a, send_b)[way].at[lax.rem(jnp.maximum(order(kind, slot + 1, way), 0), 2), units]
             return remote(
-                home, r_rs.at[kind, slot, way], rs_s.at[kind, slot, way], rs_r.at[kind, slot, way], line_goal(way)
+                home, r_rs.at[kind, slot, way, units], rs_s.at[kind, slot, way, part], rs_r.at[kind, slot, way, part],
+                line_goal(way),
             )
 
         def unit_sent(number, way):
-            unit_copy(turn_of(jnp.maximum(number, 0), way), way).wait_send()
-
-        def unit_slot(turn):
+            for part in range(2):
+                unit_copy(turn_of(jnp.maximum(number, 0), way), way, part).wait_send()
+
+        def unit_slot(turn, part):
             kind, slot = lax.div(turn, LINE - 1), lax.rem(turn, LINE - 1) + 1
             own, other = unit_terms(kind)
+            start, size = spans[part]
+            cut = slice(start, start + size)
             for way in range(2):
 
                 @pl.when(goes(slot, way))
                 def _():
                     number = order(kind, slot, way)
                     home = (send_a, send_b)[way].at[lax.rem(jnp.maximum(number, 0), 2)]
-                    pl.when(number >= 2)(lambda: unit_sent(number - 2, way))
+                    if part == 0:
+                        pl.when(number >= 2)(lambda: unit_sent(number - 2, way))
                     place = LINE - slot + z if way == 0 else slot - LINE + z
-                    outer_product(home, 0, place, own, other)
+                    home[cut, :] = dot(own[cut, :], cols_own[place]) + dot(other[cut, :], hidden_theirs[place])
 
                     @pl.when((slot > 1) & inner_place(way))
                     def _():
                         before = jnp.maximum(turn - 1, 0)
-                        unit_copy(before, way).wait_recv()
-                        landed = r_rs.at[lax.div(before, LINE - 1), lax.rem(before, LINE - 1), way]
-                        moved([(landed, stage.at[way])])
-                        home[...] = home[...] + stage[way]
-
-                    unit_copy(turn, way).start()
+                        unit_copy(before, way, part).wait_recv()
+                        landed = r_rs.at[lax.div(before, LINE - 1), lax.rem(before, LINE - 1), way, pl.ds(start, size)]
+                        moved([(landed, stage.at[way, pl.ds(start, size)])])
+                        home[cut, :] = home[cut, :] + stage[way, cut, :]
+
+                    unit_copy(turn, way, part).start()
 
         def unit_end(kind):
             own, other = unit_terms(kind)
@@ -875,21 +905,25 @@
 
                 @pl.when(inner_place(way))
                 def _():
-                    unit_copy(kind * (LINE - 1) + LINE - 2, way).wait_recv()
+                    for part in range(2):
+                        unit_copy(kind * (LINE - 1) + LINE - 2, way, part).wait_recv()
                     moved([(r_rs.at[kind, LINE - 2, way], stage.at[1])])
                     stage[0] = stage[0] + stage[1]
 
             moved([(stage.at[0], (out_gate, out_up)[kind])])
 
         def late_home(slot, way):
-            number = jnp.maximum(order(2, slot, way), 0)
-            return (send_a, send_b)[way].at[lax.rem(number, 2), pl.ds(0, inner)]
+            return parts.at[:, way, :, pl.ds(block * (slot - 1), block)]
 
         def late_copy(slot, way):
             return remote(
-                late_home(slot, way), r_rsd.at[slot - 1, way], rs_s.at[2, slot - 1, way], rs_r.at[2, slot - 1, way],
-                line_goal(way),
+                late_home(slot, way), r_rsd.at[slot - 1, way], rs_s.at[2, slot - 1, way, 0],
+                rs_r.at[2, slot - 1, way, 0], line_goal(way),
             )
+
+        def late_product(place, piece):
+            cut = slice(piece * rows, (piece + 1) * rows)
+            return dot(att_turned[cut, :], late_own[place]) + dot(att_theirs[cut, :], late_theirs[place])
 
         def late_slot(slot):
             for way in range(2):
@@ -897,32 +931,24 @@
                 @pl.when(goes(slot, way))
                 def _():
                     home = late_home(slot, way)
-                    number = order(2, slot, way)
-                    of_units = number - 2 < 2 * count(way)
-                    pl.when(of_units)(lambda: unit_sent(number - 2, way))
-                    if slot == LINE - 1:
-                        pl.when(~of_units)(lambda: late_copy(slot - 2, way).wait_send())
                     place = LINE - slot + z if way == 0 else slot - LINE + z
-                    outer_product(home, 1, place, att_turned, att_theirs)
+                    for piece in range(CHUNKS):
+                        home[piece] = late_product(place, piece)
                     if slot > 1:
 
                         @pl.when(inner_place(way))
                         def _():
                             late_copy(slot - 1, way).wait_recv()
-                            arrived = stage.at[way, pl.ds(0, inner)]
+                            arrived = blocks.at[pl.ds(0, CHUNKS)]
                             moved([(r_rsd.at[slot - 2, way], arrived)])
                             home[...] = home[...] + arrived[...]
 
                     late_copy(slot, way).start()
 
-        def last_sent(way):
-            pl.when(goes(LINE - 1, way))(lambda: late_copy(LINE - 1, way).wait_send())
-            pl.when(goes(LINE - 2, way))(lambda: late_copy(LINE - 2, way).wait_send())
-            pl.when(count(way) == 1)(lambda: unit_sent(1, way))
-
         def late_end():
-            total, arrived = stage.at[0, pl.ds(0, inner)], stage.at[1, pl.ds(0, inner)]
-            outer_product(total, 1, z, att_turned, att_theirs)
+            total, arrived = blocks.at[pl.ds(0, CHUNKS)], blocks.at[pl.ds(CHUNKS, CHUNKS)]
+            for piece in range(CHUNKS):
+                total[piece] = late_product(z, piece)
             for way in range(2):
 
                 @pl.when(inner_place(way))
@@ -931,10 +957,16 @@
                     moved([(r_rsd.at[LINE - 2, way], arrived)])
                     total[...] = total[...] + arrived[...]
 
-            gbuf[0:block, :] = total[...].T
+            for piece in range(CHUNKS):
+                gbuf[0:block, piece * rows : (piece + 1) * rows] = total[piece].T
             moved([(gbuf.at[pl.ds(0, block)], out_dense)])
+
+        def last_sent():
             for way in range(2):
-                last_sent(way)
+                for slot in range(1, LINE):
+                    pl.when(goes(slot, way))(late_copy(slot, way).wait_send)
+                pl.when(count(way) > 0)(lambda: unit_sent(2 * count(way) - 1, way))
+                pl.when(count(way) > 0)(lambda: unit_sent(2 * count(way) - 2, way))
 
         def attention_backward(place, carried):
             hot_t = hot_turned[...]
@@ -1085,29 +1117,21 @@
                 act_take(1, chunk)
                 act_send(2, chunk)
 
-        def down_all():
-            down_products()
-            down_copy().start()
-
         at_end = (z == 0) | (z == LINE - 1)
 
-        for chunk in range(CHUNKS):
-            cols_copy(0, chunk).wait()
-        fetch_columns(0)
-        for chunk in range(CHUNKS):
-            pair_copy(0, chunk).wait()
-        pair_copy(1, 0).start()
-        pair_copy(1, 1).start()
-        fetch_rows(r_y.at[0], theirs.at[1])
         for chunk in range(CHUNKS):
             for way in range(2):
                 active, copy = act_copy(way, 0, chunk)
                 pl.when(active)(copy.wait_send)
         def one_turn(turn, carried):
-            unit_slot(turn)
+            for part in range(2):
+                pl.when(turn == 0)(lambda: fetch_units(0, part))
+                unit_slot(turn, part)
 
             @pl.when(turn == 0)
             def _():
+                pair_send(1, 0)
+                pair_send(1, 1)
                 for chunk in range(CHUNKS):
                     act_take(0, chunk)
                     act_send(1, chunk)
@@ -1118,45 +1142,57 @@
                 small_sums()
                 pl.when(~at_end)(act_pass)
                 sums_first()
-                pair_copy(1, 2).start()
-                pair_copy(1, 3).start()
                 for chunk in range(CHUNKS):
                     cols_copy(1, chunk).start()
+                pair_send(1, 2)
+                pair_send(1, 3)
 
             @pl.when(turn == 2)
             def _():
+                sums_near()
                 for chunk in range(CHUNKS):
-                    pair_copy(1, chunk).wait()
-                fetch_rows(r_y.at[1], theirs.at[2])
-
-            pl.when(turn == 3)(sums_near)
-            pl.when((turn == 3) & ~at_end | (turn == 5) & at_end)(down_all)
-            pl.when(turn == 4)(sums_far)
+                    cols_copy(1, chunk).wait()
+                fetch_columns(1, late_theirs)
+                fetch_rows(r_att, att_theirs)
+                late_slot(1)
+
+            lately = (turn == 3) & ~at_end | (turn == 2) & at_end
+            pl.when(lately)(lambda: late_slot(2))
+            pl.when((turn == 3) & ~at_end | (turn == 4) & at_end)(down_products)
+            pl.when(lately)(lambda: late_slot(3))
+
+            @pl.when(turn == 2)
+            def _():
+                for part in range(2):
+                    fetch_units(1, part)
+
+            @pl.when((turn == 3) & ~at_end | (turn == 5) & at_end)
+            def _():
+                sums_far()
+                sums_middle()
+                down_copy().start()
+
+            @pl.when((turn == 4) & ~at_end | (turn == 5) & at_end)
+            def _():
+                sums_end()
+                head_gradients()
+                table_part()
+
             return carried
 
         lax.fori_loop(0, 2 * (LINE - 1), one_turn, 0)
         unit_end(0)
-        for chunk in range(CHUNKS):
-            cols_copy(1, chunk).wait()
-        fetch_columns(1)
-        fetch_rows(r_att, att_theirs)
-        late_slot(1)
-        sums_middle()
-        sums_end()
-        head_gradients()
-        table_part()
-        late_slot(2)
+        late_end()
         table_middle()
-        unit_end(1)
-        late_slot(3)
         table_end()
         down_end()
-        late_end()
+        unit_end(1)
+        last_sent()
 
     pl.run_scoped(
         last_scope,
         pltpu.VMEM((3, local_hidden, length), LOW),
-        pltpu.VMEM((2, LINE, length, block), LOW),
+        pltpu.VMEM((LINE, length, block), LOW),
         pltpu.VMEM((2, length, block), LOW),
         pltpu.VMEM((inner, length), LOW),
         pltpu.VMEM((2, local_hidden, block), FULL),
@@ -1202,7 +1238,7 @@
     angles = np.arange(length)[:, None] * frequency[None, :]
     cosine = np.concatenate([np.cos(angles)] * 2, axis=1).astype(np.float32)
     sine = np.concatenate([-np.sin(angles), np.sin(angles)], axis=1).astype(np.float32)
-    norms = jnp.stack([norm1_gain, norm1_bias, norm2_gain, norm2_bias])
+    norms = [vector.reshape(1, width) for vector in (norm1_gain, norm1_bias, norm2_gain, norm2_bias)]
 
     hbm = pl.BlockSpec(memory_space=pl.ANY)
     vmem = pl.BlockSpec(memory_space=pltpu.VMEM)
@@ -1229,7 +1265,7 @@
         ((CHUNKS, length, inner), FULL),
         ((local_hidden, block), FULL),
         ((2, LINE - 1, 2, local_hidden, block), FULL),
-        ((LINE - 1, 2, inner, block), FULL),
+        ((LINE - 1, 2, CHUNKS, rows, block), FULL),
         ((4, sums_rows, width // 2), FULL),
     ]
     scratch = [
@@ -1247,6 +1283,7 @@
         ((2, local_hidden, block), FULL),
         ((LINE, length, block), LOW),
         ((2, CHUNKS, rows, block), FULL),
+        ((LINE, length, block), LOW),
         ((2, length, block), LOW),
         ((LINE, CHUNKS, rows, block), FULL),
         ((length, inner), LOW),
@@ -1264,13 +1301,13 @@
     each = (3, CHUNKS)
     semaphores = [
         each, each, each, each, each, each, (2, LINE - 1, CHUNKS), (2, LINE - 1, CHUNKS), each, each, (3,), (3,),
-        (2, CHUNKS), (2, CHUNKS), (2,), (2,), (2, CHUNKS), (2, CHUNKS), None, None, None, None,
-        (3, LINE - 1, 2), (3, LINE - 1, 2), (4,), (4,), (2,), (2,), (4,), (4,),
+        (2, CHUNKS), (2, CHUNKS), (2,), (2,), (2, CHUNKS, 2), (2, CHUNKS, 2), None, None, None, None,
+        (3, LINE - 1, 2, 2), (3, LINE - 1, 2, 2), (4,), (4,), (2,), (2,), (4,), (4,),
     ]
     results = pl.pallas_call(
         functools.partial(layer_kernel, length, width, local_hidden),
         out_shape=[jax.ShapeDtypeStruct(shape, dtype) for shape, dtype in shapes],
-        in_specs=[smem] * 2 + [vmem] * 5 + [hbm] * 8,
+        in_specs=[smem] * 2 + [vmem] * 8 + [hbm] * 8,
         out_specs=[hbm] * len(shapes),
         scratch_shapes=[pltpu.VMEM(shape, dtype) for shape, dtype in scratch]
         + [dma if shape is None else dma(shape) for shape in semaphores],
@@ -1284,7 +1321,7 @@
         embedding,
         cosine,
         sine,
-        norms,
+        *norms,
         w_query,
         w_key,
         w_value,

time: 400 us -> 382 us (0.955)
  Pallas kernels: 380 us -> 363 us
    pallas_call x1, Pallas kernels: 380 us -> 363 us  [local_fast(): pl.pallas_call(functools.partial(layer_kernel, length, width, local_hidde...]
where the time goes in v1:
time: 382 us; the launch traced here: 377 us
  Pallas kernels  363 us (95%)
  local copies, waits for them, and re-layouts  12.6 us (3%)
    pallas_call x1, Pallas kernels, local_fast(): pl.pallas_call(functools.partial(layer_kernel, length, width, local_hidde...  363 us
    unnamed x25, local copies, waits for them, and re-layouts  11.1 us

profile of v1, /device:TPU:30, one launch (start us, length us, event | category | flops | bytes accessed | tf_op | source)
XLA Modules:
  0.0 377.2 jit_solution(13297228075719851929)
XLA Ops:
  1.3 363.4 %shard_map.273 = (bf16[512,2048]{1,0:T(8,128)(2,1)}, f32[16,2048]{1,0:T(8,128)}, f32[256,512]{1,0:T(8,128)}, f32[256,512]{1,0:T(8,128)}, f32[256,512]{1,0:T(8,12...) custom-call(s32[1]{0:T(128)S(6)} %copy.40.prefix_ref, ...), custom_call_target="tpu_custom_call" | custom-call | tf_op jit(solution)/shard_map/pallas_call | solution.py:1307
  364.7 1.4 fusion
  366.1 0.0 copy-start.7
  366.1 0.0 copy-start.6
  366.1 0.0 copy-start.5
  366.1 3.3 copy.41
  369.4 0.0 copy-done.7
  369.4 0.0 copy-start.4
  369.4 0.0 copy-start.3
  369.4 0.7 copy.42
  370.0 0.0 copy-done.6
  370.0 0.0 copy-start.2
  370.0 0.8 copy.43
  370.8 0.0 copy-done.5
  370.8 0.8 copy.44
  371.6 0.0 copy-done.4
  371.6 0.8 copy.45
  372.4 0.0 copy-done.3
  372.4 0.0 copy-start.1
  372.4 0.8 copy.46
  373.2 0.0 copy-done.2
  373.2 1.1 copy.47
  374.3 0.0 copy-done.1
  374.3 0.0 copy-start
  374.3 1.1 copy.48
  375.4 0.8 copy-done
  376.2 1.1 copy.49
Async XLA Ops:
  366.1 3.3 copy-start.7
  366.1 3.9 %copy-start.6 = (f32[256,512]{1,0:T(8,128)S(1)}, f32[256,512]{1,0:T(8,128)}, u32[]{:S(2)}) copy-start(f32[256,512]{1,0:T(8,128)} %get-tuple-element.52) | copy-start | bytes 1572868
  366.1 4.7 %copy-start.5 = (f32[256,512]{1,0:T(8,128)S(1)}, f32[256,512]{1,0:T(8,128)}, u32[]{:S(2)}) copy-start(f32[256,512]{1,0:T(8,128)} %get-tuple-element.53) | copy-start | bytes 1572868
  369.4 2.3 copy-start.4
  369.4 3.1 copy-start.3
  370.0 3.2 copy-start.2
  372.4 1.9 copy-start.1
  374.3 1.9 copy-start

commit v2 on v1

--- a/solution.py
+++ b/solution.py
@@ -514,11 +514,12 @@
     def every_chunk(body):
         lax.fori_loop(0, CHUNKS, lambda chunk, carried: (body(chunk), carried)[1], 0)
 
-    column = lax.broadcasted_iota(jnp.int32, (length, length), 1)
-    row = lax.broadcasted_iota(jnp.int32, (length, length), 0)
     score_scale = 1.0 / math.sqrt(HD)
 
-    def probabilities(queries, keys):
+    def probabilities(queries, keys, begin):
+        shape = (queries.shape[0], length)
+        column = lax.broadcasted_iota(jnp.int32, shape, 1)
+        row = lax.broadcasted_iota(jnp.int32, shape, 0) + begin
         visible = (column < prefix_ref[0]) | (column <= row)
         scores = jnp.where(visible, dot_nt(queries, keys) * score_scale, -1e30)
         weights = jnp.exp(scores - jnp.max(scores, axis=-1, keepdims=True))
@@ -555,30 +556,33 @@
             for place in range(heads_here):
                 tab[kind * heads_here + place] = table[:, place * HD : (place + 1) * HD]
 
-        def attend_head(place, carried):
+        def head_inputs(place, carried):
             hot = one_hot[...]
             lin = []
             for kind in range(3):
                 high, rest = split_low(tab[kind * heads_here + place])
                 lin.append(dot(hot, high) + dot(hot, rest))
-            queries = turn_by(lin[0], sin_ref[...]).astype(LOW)
-            keys = turn_by(lin[1], sin_ref[...]).astype(LOW)
-            values = lin[2].astype(LOW)
-            heads[0, place], heads[1, place], heads[2, place] = queries, keys, values
-            probability = probabilities(queries, keys).astype(LOW)
-            mixed = dot(probability, values).astype(LOW)
-            att_low[:, head_lanes(place)] = mixed
-            turned = mixed.astype(FULL).T
-            head_rows = pl.ds(pl.multiple_of(place * HD, HD), HD)
-            att_turned[head_rows, :] = turned.astype(LOW)
-            gbuf[head_rows, :] = turned
+            heads[0, place] = turn_by(lin[0], sin_ref[...]).astype(LOW)
+            heads[1, place] = turn_by(lin[1], sin_ref[...]).astype(LOW)
+            heads[2, place] = lin[2].astype(LOW)
             return carried
 
-        lax.fori_loop(0, heads_here, attend_head, 0)
-        loads[3].wait()
-        pl.semaphore_wait(barrier, len(greeted))
+        lax.fori_loop(0, heads_here, head_inputs, 0)
+
+        def attend(chunk):
+            for place in range(heads_here):
+                queries = heads[0, place, chunk_rows(chunk), :]
+                probability = probabilities(queries, heads[1, place], chunk * rows).astype(LOW)
+                mixed = dot(probability, heads[2, place]).astype(LOW)
+                att_low[chunk_rows(chunk), place * HD : (place + 1) * HD] = mixed
+                turned = mixed.astype(FULL).T
+                att_turned[place * HD : (place + 1) * HD, chunk_lanes(chunk)] = turned.astype(LOW)
+                gbuf[place * HD : (place + 1) * HD, chunk_lanes(chunk)] = turned
 
         def project(chunk):
+            attend(chunk)
+            pl.when(chunk == 0)(lambda: loads[3].wait())
+            pl.when(chunk == 0)(lambda: pl.semaphore_wait(barrier, len(greeted)))
             mixed = att_low[chunk_rows(chunk), :]
 
             def columns(start, size):
@@ -898,7 +902,8 @@
 
                     unit_copy(turn, way, part).start()
 
-        def unit_end(kind):
+        def unit_end():
+            kind = 0
             own, other = unit_terms(kind)
             outer_product(stage.at[0], 0, z, own, other)
             for way in range(2):
@@ -910,7 +915,17 @@
                     moved([(r_rs.at[kind, LINE - 2, way], stage.at[1])])
                     stage[0] = stage[0] + stage[1]
 
-            moved([(stage.at[0], (out_gate, out_up)[kind])])
+            moved([(stage.at[0], out_gate)])
+
+        def last_product():
+            own, other = unit_terms(1)
+            outer_product(stage.at[0], 0, z, own, other)
+            moved([(stage.at[0], out_up)])
+
+        def last_landed():
+            for way in range(2):
+                for part in range(2):
+                    pl.when(inner_place(way))(unit_copy(2 * LINE - 3, way, part).wait_recv)
 
         def late_home(slot, way):
             return parts.at[:, way, :, pl.ds(block * (slot - 1), block)]
@@ -972,7 +987,7 @@
             hot_t = hot_turned[...]
             queries, keys, values = heads[0, place], heads[1, place], heads[2, place]
             grad_mixed = grad_att[place]
-            probability = probabilities(queries, keys)
+            probability = probabilities(queries, keys, 0)
             grad_prob = dot_nt(grad_mixed, values)
             centre = jnp.sum(grad_prob * probability, axis=-1, keepdims=True)
             grad_scores = (probability * (grad_prob - centre)).astype(LOW)
@@ -1181,12 +1196,13 @@
             return carried
 
         lax.fori_loop(0, 2 * (LINE - 1), one_turn, 0)
-        unit_end(0)
+        unit_end()
+        last_product()
         late_end()
         table_middle()
         table_end()
         down_end()
-        unit_end(1)
+        last_landed()
         last_sent()
 
     pl.run_scoped(
@@ -1206,6 +1222,63 @@
         pltpu.VMEM(r_sums.shape[1:], FULL),
         pltpu.VMEM(cols_own.shape, LOW),
     )
+
+
+def write_kernel(*refs):
+    count = 10
+    late = 7
+    sources, landed = refs[:count], refs[count]
+    targets = refs[count + 1 : 2 * count + 4]
+    rooms, terms, first_sem, second_sem = refs[2 * count + 4 : 3 * count + 4], *refs[3 * count + 4 : 3 * count + 7]
+    z = lax.div(lax.axis_index("dp"), 2)
+    order = [late] + [place for place in range(count) if place != late]
+    loads = {
+        place: pltpu.make_async_copy(sources[place], rooms[place], first_sem.at[place]) for place in range(count)
+    }
+    more = [
+        pltpu.make_async_copy(landed.at[1, LINE - 2, way], terms.at[way], first_sem.at[count + way]) for way in range(2)
+    ]
+    for copy in more:
+        copy.start()
+    for place in order:
+        loads[place].start()
+    stores = []
+    for copy in more:
+        copy.wait()
+    for place in order:
+        loads[place].wait()
+        room = rooms[place]
+        if place == late:
+            for way, active in ((0, z > 0), (1, z < LINE - 1)):
+
+                @pl.when(active)
+                def _():
+                    room[...] = room[...] + terms[way]
+
+        if place < count - 1:
+            stores.append(pltpu.make_async_copy(room, targets[place], second_sem.at[place]))
+            stores[-1].start()
+        else:
+            for vector in range(4):
+                targets[place + vector][...] = room[vector : vector + 1, :]
+    for copy in stores:
+        copy.wait()
+
+
+def write_out(results, landed):
+    hbm = pl.BlockSpec(memory_space=pl.ANY)
+    rows = jax.ShapeDtypeStruct((1, results[-1].shape[1]), FULL)
+    shapes = [jax.ShapeDtypeStruct(value.shape, value.dtype) for value in results[:-1]] + [rows] * 4
+    return pl.pallas_call(
+        write_kernel,
+        out_shape=shapes,
+        in_specs=[hbm] * (len(results) + 1),
+        out_specs=[hbm] * (len(results) - 1) + [pl.BlockSpec(memory_space=pltpu.VMEM)] * 4,
+        scratch_shapes=[pltpu.VMEM(value.shape, value.dtype) for value in results]
+        + [pltpu.VMEM((2,) + results[7].shape, FULL)]
+        + [pltpu.SemaphoreType.DMA((len(results) + 2,))] * 2,
+        compiler_params=pltpu.CompilerParams(vmem_limit_bytes=62 * 2**20),
+    )(*results, landed)
 
 
 def local_fast(
@@ -1331,7 +1404,9 @@
         w_down.T,
         cotangent,
     )
-    block_out, table, out_query, out_key, out_value, out_dense, out_gate, out_up, out_down, out_norms = results[:10]
+    written = write_out(results[:10], results[18])
+    block_out, table, out_query, out_key, out_value, out_dense, out_gate, out_up, out_down = written[:9]
+    out_norms = written[9:]
     return (
         block_out,
         table,
@@ -1342,10 +1417,10 @@
         out_gate.T,
         out_up.T,
         out_down.T,
-        out_norms[0],
-        out_norms[1],
-        out_norms[2],
-        out_norms[3],
+        out_norms[0].reshape(width // (2 * LINE)),
+        out_norms[1].reshape(width // (2 * LINE)),
+        out_norms[2].reshape(width // (2 * LINE)),
+        out_norms[3].reshape(width // (2 * LINE)),
     )
 
 

time: 382 us -> 373 us (0.976)
  local copies, waits for them, and re-layouts: 12.6 us -> 0 us
  Pallas kernels: 363 us -> 367 us
    unnamed x25 -> x0, local copies, waits for them, and re-layouts: 11.1 us -> none
    pallas_call x0 -> x1, Pallas kernels: none -> 8.32 us  [write_out(): pl.pallas_call(write_kernel, out_shape=shapes, in_specs=[hbm] * (len(resu...]
    pallas_call x1, Pallas kernels: 363 us -> 358 us  [local_fast(): pl.pallas_call(functools.partial(layer_kernel, length, width, local_hidde...]
where the time goes in v2:
time: 373 us; the launch traced here: 368 us
  Pallas kernels  367 us (98%)
    pallas_call x1, Pallas kernels, local_fast(): pl.pallas_call(functools.partial(layer_kernel, length, width, local_hidde...  358 us
    pallas_call x1, Pallas kernels, write_out(): pl.pallas_call(write_kernel, out_shape=shapes, in_specs=[hbm] * (len(resu...  8.32 us

profile of v2, /device:TPU:30, one launch (start us, length us, event | category | flops | bytes accessed | tf_op | source)
XLA Modules:
  0.0 368.1 jit_solution(14531875877699254794)
XLA Ops:
  1.3 358.3 %shard_map.273 = (bf16[512,2048]{1,0:T(8,128)(2,1)}, f32[16,2048]{1,0:T(8,128)}, f32[256,512]{1,0:T(8,128)}, f32[256,512]{1,0:T(8,128)}, f32[256,512]{1,0:T(8,12...) custom-call(s32[1]{0:T(128)S(6)} %copy.31.prefix_ref, ...), custom_call_target="tpu_custom_call" | custom-call | tf_op jit(solution)/shard_map/pallas_call | solution.py:1380
  359.6 8.3 %shard_map.274 = (bf16[512,2048]{1,0:T(8,128)(2,1)}, f32[16,2048]{1,0:T(8,128)}, f32[256,512]{1,0:T(8,128)}, f32[256,512]{1,0:T(8,128)}, f32[256,512]{1,0:T(8,12...) custom-call(bf16[512,2048]{1,0:T(8,128)(2,1)} %get-tuple-element.37., ...), custom_call_target="tpu_custom_call" | custom-call | tf_op jit(solution)/shard_map/pallas_call | solution.py:1272

commit v3 on v2

--- a/solution.py
+++ b/solution.py
@@ -329,11 +329,11 @@
     prefix_ref, cluster_ref, ids_row, emb, cos_ref, sin_ref, gain_one, bias_one, gain_two, bias_two, w_query_hbm, w_key_hbm, w_value_hbm, w_dense_hbm,
     w_gate_hbm, w_up_hbm, w_down_hbm, cot_hbm,
     block_out, out_table, out_query, out_key, out_value, out_dense, out_gate, out_up, out_down, out_norms,
-    r_act, r_two, r_y, r_cols, r_att, xhat_park, grad_two_park, r_dny, r_rs, r_rsd, r_sums,
+    r_act, r_two, r_y, r_cols, r_att, xhat_park, grad_two_park, r_dny, r_rs, r_late, r_dz, r_dx, r_sums,
     parts, core_in, x_in, back_in, blocks, xbuf, gbuf, obuf, gate_up, grads_low, act_low, send_a, cols_own, cols_send,
     hidden_theirs, two_own, two_send, att_low, att_turned, heads, w_dense, one_hot, hot_turned, rstd_one, vectors, table_core, table_x,
     core_s, core_r, x_s, x_r, back_s, back_r, act_s, act_r, two_s, two_r, fwd_two_s, fwd_two_r, cols_s, cols_r, fwd_s,
-    fwd_r, ys_s, ys_r, att_s, att_r, dny_s, dny_r, rs_s, rs_r, sums_s, sums_r, table_s, table_r, load_sem, weight_sem,
+    fwd_r, ys_s, ys_r, att_s, att_r, dny_s, dny_r, late_s, late_r, dz_s, dz_r, dx_s, dx_r, rs_s, rs_r, sums_s, sums_r, table_s, table_r, load_sem, weight_sem,
 ):
     dp, mp = lax.axis_index("dp"), lax.axis_index("mp")
     z, y = lax.div(dp, 2), lax.rem(dp, 2)
@@ -358,6 +358,8 @@
     core_peer = at(core_to=1 - core)
     x_peer = at(x_to=1 - x)
     y_peer = at(y_to=1 - y)
+    z_peer = at(z_to=z + 1 - 2 * lax.rem(z, 2))
+    at_end = (z == 0) | (z == LINE - 1)
 
     def remote(source, target, send, receive, device):
         return pltpu.make_async_remote_copy(
@@ -430,21 +432,21 @@
     def half_lanes(side):
         return pl.ds(pl.multiple_of(side * block, block), block)
 
-    def keep_columns(own, chunk):
+    def keep_columns(chunk):
         for place in range(LINE):
-            own[place, chunk_rows(chunk), :] = blocks[2 * place + y].astype(LOW)
+            cols_own[place, chunk_rows(chunk), :] = blocks[2 * place + y].astype(LOW)
         for place in range(2):
-            cols_send[place, chunk] = blocks[2 * (2 * core + place) + 1 - y]
-
-    def cols_copy(kind, chunk):
+            cols_send[2 * chunk + place] = blocks[2 * (2 * core + place) + 1 - y]
+
+    def cols_copy(chunk):
         return remote(
-            cols_send.at[:, chunk], r_cols.at[kind, pl.ds(2 * core, 2), chunk],
-            cols_s.at[kind, chunk], cols_r.at[kind, chunk], y_peer,
+            cols_send.at[pl.ds(2 * chunk, 2)], r_cols.at[pl.ds(2 * core, 2), chunk],
+            cols_s.at[chunk], cols_r.at[chunk], y_peer,
         )
 
-    def forward_copy(kind):
-        view = r_cols.at[kind, pl.ds(2 * core, 2)]
-        return remote(view, view, fwd_s.at[kind], fwd_r.at[kind], core_peer)
+    def forward_copy():
+        view = r_cols.at[pl.ds(2 * core, 2)]
+        return remote(view, view, fwd_s, fwd_r, core_peer)
 
     def act_copy(way, hop, chunk):
         goal = jnp.clip(z + 1 - 2 * way, 0, LINE - 1)
@@ -473,16 +475,20 @@
             _, copy = act_copy(way, hop, chunk)
             pl.when(act_landed(way, hop))(copy.wait_recv)
 
-    def two_copy(step, chunk):
+    other_x = 2 * (1 - x) + core
+
+    def two_copy(step):
         goal = lax.rem(z + step, LINE)
         return remote(
-            two_send.at[goal, chunk], r_two.at[z, core, chunk],
-            two_s.at[step - 1, chunk], two_r.at[step - 1, chunk], at(z_to=goal),
+            two_send.at[pl.ds(2 * goal, 2)], r_two.at[z, pl.ds(2 * mp, 2)],
+            two_s.at[step - 1], two_r.at[step - 1], at(z_to=goal),
         )
 
-    def two_forward(step):
-        view = r_two.at[lax.rem(z + step, LINE), core]
-        return remote(view, view, fwd_two_s.at[step - 1], fwd_two_r.at[step - 1], core_peer)
+    def two_spread(turn, step):
+        quarter = other_x if turn == 2 else mp
+        view = r_two.at[lax.rem(z + step, LINE), pl.ds(2 * quarter, 2)]
+        device = x_peer if turn == 1 else core_peer
+        return remote(view, view, fwd_two_s.at[turn, step - 1], fwd_two_r.at[turn, step - 1], device)
 
     def pair_copy(which, chunk, part):
         units = pl.ds(*spans[part])
@@ -496,15 +502,15 @@
             pair_copy(which, chunk, part).start()
 
     def rows_copy():
-        return remote(gbuf, r_att, att_s, att_r, y_peer)
-
-    def fetch_columns(kind, target):
-        forward = forward_copy(kind)
+        return remote(gbuf, r_att, att_s, att_r, z_peer)
+
+    def fetch_columns(target):
+        forward = forward_copy()
         forward.start()
         forward.wait()
         for pair in range(2):
             moved(
-                [(r_cols.at[kind, 2 * pair + place], blocks.at[pl.ds(CHUNKS * place, CHUNKS)]) for place in range(2)]
+                [(r_cols.at[2 * pair + place], blocks.at[pl.ds(CHUNKS * place, CHUNKS)]) for place in range(2)]
             )
             for place in range(2):
                 for chunk in range(CHUNKS):
@@ -619,8 +625,8 @@
             park.start()
             hidden_low = (xhat * gain_one[...] + bias_one[...]).astype(LOW)
             put_blocks(hidden_low.astype(FULL))
-            keep_columns(cols_own, chunk)
-            cols_copy(0, chunk).start()
+            keep_columns(chunk)
+            cols_copy(chunk).start()
 
             def units_tile(start, size):
                 cut = pl.ds(start, size)
@@ -682,10 +688,13 @@
             put_blocks(grad_low.astype(FULL))
             for place in range(2):
                 two_own[place, chunk_rows(chunk), :] = blocks[2 * z + place].astype(LOW)
-            for place in range(LINE):
-                two_send[place, chunk] = blocks[2 * place + core]
-            for step in range(1, LINE):
-                two_copy(step, chunk).start()
+
+            @pl.when(chunk == mp)
+            def _():
+                two_send[...] = blocks[...]
+                for step in range(1, LINE):
+                    two_copy(step).start()
+
 
             def units_tile(start, size):
                 cut = pl.ds(start, size)
@@ -717,12 +726,20 @@
 
         def take_hidden():
             for chunk in range(CHUNKS):
-                cols_copy(0, chunk).wait()
-            fetch_columns(0, hidden_theirs)
+                cols_copy(chunk).wait()
+            fetch_columns(hidden_theirs)
 
         def step(turn, carried):
             pl.when(turn == CHUNKS - 1)(lambda: hidden_part(0))
-            pl.when(turn == CHUNKS)(take_hidden)
+            @pl.when(turn == CHUNKS)
+            def _():
+                for chunk in range(2):
+                    send_part(2, chunk)
+                take_hidden()
+                for chunk in range(CHUNKS - 1):
+                    act_take(0, chunk)
+                    act_send(1, chunk)
+
             pl.when(turn < CHUNKS)(lambda: feed_forward(turn))
             pl.when(turn == 1)(lambda: rows_copy().wait())
             pl.when(turn > 0)(lambda: feed_backward(turn - 1))
@@ -731,7 +748,8 @@
         lax.fori_loop(0, CHUNKS + 1, step, 0)
 
         hidden_part(1)
-        every_chunk(lambda chunk: send_part(2, chunk))
+        for chunk in range(2, CHUNKS):
+            send_part(2, chunk)
 
     pl.run_scoped(
         middle_scope,
@@ -759,7 +777,14 @@
                 grad_one_own[chunk_rows(chunk), place * block : (place + 1) * block] = blocks[2 * mp + place]
             grad_low = grad_one.astype(LOW)
             put_blocks(grad_low.astype(FULL))
-            keep_columns(late_own, chunk)
+            for place in range(2 * LINE):
+                late_own[place, chunk_rows(chunk), :] = blocks[place].astype(LOW)
+
+            @pl.when(chunk == mp)
+            def _():
+                for place in range(2 * LINE):
+                    cols_send[place] = blocks[place]
+
             grad_mixed = dot(grad_low, w_dense[...]).astype(LOW)
             for place in range(heads_here):
                 grad_att[place, chunk_rows(chunk), :] = grad_mixed[:, place * HD : (place + 1) * HD]
@@ -782,8 +807,8 @@
             for place in range(2):
                 target[:, block * place : block * (place + 1)] = views[place][...].astype(LOW)
 
-        def outer_product(target, kind, place, own, other):
-            right, right_theirs = (cols_own, late_own)[kind][place], (hidden_theirs, late_theirs)[kind][place]
+        def outer_product(target, place, own, other):
+            right, right_theirs = cols_own[place], hidden_theirs[place]
 
             def rows_tile(start, size):
                 cut = pl.ds(start, size)
@@ -793,27 +818,21 @@
 
         def down_products():
             for step in range(1, LINE):
-                for chunk in range(CHUNKS):
-                    two_copy(step, chunk).wait()
+                two_spread(1, step).wait()
+                two_spread(2, step).start()
             for step in range(1, LINE):
-                two_forward(step).start()
-            for step in range(1, LINE):
-                two_forward(step).wait()
+                two_spread(0, step).wait()
+                two_spread(2, step).wait()
             for chunk in range(CHUNKS):
                 pl.when(at_end)(lambda: act_take(1, chunk))
                 act_take(2, chunk)
             for step in range(LINE):
                 owner = lax.rem(z + step, LINE)
                 if step:
-                    moved(
-                        [
-                            (r_two.at[owner, place], blocks.at[pl.ds(CHUNKS * place, CHUNKS)])
-                            for place in range(2)
-                        ]
-                    )
+                    moved([(r_two.at[owner], blocks)])
                     for place in range(2):
                         for chunk in range(CHUNKS):
-                            piece = blocks[CHUNKS * place + chunk].astype(LOW)
+                            piece = blocks[2 * chunk + place].astype(LOW)
                             two_theirs[place, chunk * rows : (chunk + 1) * rows, :] = piece
                     fetch_rows(r_act.at[owner], theirs.at[0])
                 left, right = (theirs.at[0], two_theirs) if step else (act_low, two_own)
@@ -841,11 +860,14 @@
                         active, copy = act_copy(way, hop, chunk)
                         pl.when(active)(copy.wait_send)
 
+        def toward(side):
+            return jnp.where(z < LINE // 2, side, 1 - side)
+
         def goes(slot, way):
-            return z < slot if way == 0 else z > LINE - 1 - slot
+            return jnp.where(way == 0, z < slot, z > LINE - 1 - slot)
 
         def inner_place(way):
-            return z > 0 if way == 0 else z < LINE - 1
+            return jnp.where(way == 0, z > 0, z < LINE - 1)
 
         def line_goal(way):
             return at(z_to=jnp.clip(z + 1 - 2 * way, 0, LINE - 1))
@@ -854,7 +876,7 @@
             return grads_low.at[pl.ds(pl.multiple_of(kind * shift, 16), local_hidden)], theirs.at[1 + kind]
 
         def count(way):
-            return LINE - 1 - z if way == 0 else z
+            return jnp.where(way == 0, LINE - 1 - z, z)
 
         def order(kind, slot, way):
             return kind * count(way) + slot - (LINE - count(way))
@@ -863,125 +885,182 @@
             many = jnp.maximum(count(way), 1)
             return lax.div(number, many) * (LINE - 1) + lax.rem(number, many) + LINE - 1 - count(way)
 
-        def unit_copy(turn, way, part):
+        def unit_copy(turn, side, part):
+            way = toward(side)
             kind, slot = lax.div(turn, LINE - 1), lax.rem(turn, LINE - 1)
             units = pl.ds(*spans[part])
-            home = (send_a, send_b)[way].at[lax.rem(jnp.maximum(order(kind, slot + 1, way), 0), 2), units]
+            home = (send_a, send_b)[side].at[lax.rem(jnp.maximum(order(kind, slot + 1, way), 0), 2), units]
             return remote(
                 home, r_rs.at[kind, slot, way, units], rs_s.at[kind, slot, way, part], rs_r.at[kind, slot, way, part],
                 line_goal(way),
             )
 
-        def unit_sent(number, way):
+        def unit_sent(number, side):
             for part in range(2):
-                unit_copy(turn_of(jnp.maximum(number, 0), way), way, part).wait_send()
-
-        def unit_slot(turn, part):
+                unit_copy(turn_of(jnp.maximum(number, 0), toward(side)), side, part).wait_send()
+
+        def unit_slot(turn, part, side):
+            way = toward(side)
             kind, slot = lax.div(turn, LINE - 1), lax.rem(turn, LINE - 1) + 1
             own, other = unit_terms(kind)
             start, size = spans[part]
             cut = slice(start, start + size)
-            for way in range(2):
-
-                @pl.when(goes(slot, way))
+
+            @pl.when(goes(slot, way))
+            def _():
+                number = order(kind, slot, way)
+                home = (send_a, send_b)[side].at[lax.rem(jnp.maximum(number, 0), 2)]
+                if part == 0:
+                    pl.when(number >= 2)(lambda: unit_sent(number - 2, side))
+                place = jnp.where(way == 0, LINE - slot + z, slot - LINE + z)
+                home[cut, :] = dot(own[cut, :], cols_own[place]) + dot(other[cut, :], hidden_theirs[place])
+
+                @pl.when((slot > 1) & inner_place(way))
                 def _():
-                    number = order(kind, slot, way)
-                    home = (send_a, send_b)[way].at[lax.rem(jnp.maximum(number, 0), 2)]
-                    if part == 0:
-                        pl.when(number >= 2)(lambda: unit_sent(number - 2, way))
-                    place = LINE - slot + z if way == 0 else slot - LINE + z
-                    home[cut, :] = dot(own[cut, :], cols_own[place]) + dot(other[cut, :], hidden_theirs[place])
-
-                    @pl.when((slot > 1) & inner_place(way))
-                    def _():
-                        before = jnp.maximum(turn - 1, 0)
-                        unit_copy(before, way, part).wait_recv()
-                        landed = r_rs.at[lax.div(before, LINE - 1), lax.rem(before, LINE - 1), way, pl.ds(start, size)]
-                        moved([(landed, stage.at[way, pl.ds(start, size)])])
-                        home[cut, :] = home[cut, :] + stage[way, cut, :]
-
-                    unit_copy(turn, way, part).start()
+                    before = jnp.maximum(turn - 1, 0)
+                    unit_copy(before, side, part).wait_recv()
+                    landed = r_rs.at[lax.div(before, LINE - 1), lax.rem(before, LINE - 1), way, pl.ds(start, size)]
+                    moved([(landed, stage.at[side, pl.ds(start, size)])])
+                    home[cut, :] = home[cut, :] + stage[side, cut, :]
+
+                unit_copy(turn, side, part).start()
 
         def unit_end():
-            kind = 0
-            own, other = unit_terms(kind)
-            outer_product(stage.at[0], 0, z, own, other)
-            for way in range(2):
-
-                @pl.when(inner_place(way))
+            own, other = unit_terms(0)
+            outer_product(stage.at[0], z, own, other)
+            for side in range(2):
+
+                @pl.when(inner_place(toward(side)))
                 def _():
                     for part in range(2):
-                        unit_copy(kind * (LINE - 1) + LINE - 2, way, part).wait_recv()
-                    moved([(r_rs.at[kind, LINE - 2, way], stage.at[1])])
+                        unit_copy(LINE - 2, side, part).wait_recv()
+                    moved([(r_rs.at[0, LINE - 2, toward(side)], stage.at[1])])
                     stage[0] = stage[0] + stage[1]
 
             moved([(stage.at[0], out_gate)])
 
         def last_product():
             own, other = unit_terms(1)
-            outer_product(stage.at[0], 0, z, own, other)
+            outer_product(stage.at[0], z, own, other)
             moved([(stage.at[0], out_up)])
 
         def last_landed():
-            for way in range(2):
+            for side in range(2):
                 for part in range(2):
-                    pl.when(inner_place(way))(unit_copy(2 * LINE - 3, way, part).wait_recv)
-
-        def late_home(slot, way):
-            return parts.at[:, way, :, pl.ds(block * (slot - 1), block)]
-
-        def late_copy(slot, way):
-            return remote(
-                late_home(slot, way), r_rsd.at[slot - 1, way], rs_s.at[2, slot - 1, way, 0],
-                rs_r.at[2, slot - 1, way, 0], line_goal(way),
-            )
-
-        def late_product(place, piece):
-            cut = slice(piece * rows, (piece + 1) * rows)
-            return dot(att_turned[cut, :], late_own[place]) + dot(att_theirs[cut, :], late_theirs[place])
-
-        def late_slot(slot):
-            for way in range(2):
-
-                @pl.when(goes(slot, way))
+                    pl.when(inner_place(toward(side)))(unit_copy(2 * LINE - 3, side, part).wait_recv)
+
+        first = jnp.where(z == 1, 2, jnp.where(z == LINE - 1, 2 * LINE - 2, 0))
+        peer_first = jnp.where(z == 0, 2, jnp.where(z == 2, 2 * LINE - 2, 0))
+        many = 2 * LINE - 2
+        def late_copy(begin, size, part):
+            span = pl.ds(begin + part * (size // 2), size // 2)
+            return remote(cols_send.at[span], r_late.at[mp, span], late_s.at[0, part], late_r.at[0, part], z_peer)
+
+        def late_send():
+            for part in range(2):
+                pl.when(at_end)(lambda: late_copy(peer_first, many, part).start())
+                pl.when(~at_end)(lambda: late_copy(peer_first, 2, part).start())
+
+        def spread_copy(turn, size, part):
+            place = other_x if turn == 3 else mp
+            view = r_late.at[place, pl.ds(first + part * (size // 2), size // 2)]
+            device = x_peer if turn == 2 else core_peer
+            return remote(view, view, late_s.at[turn, part], late_r.at[turn, part], device)
+
+        def by_size(body):
+            pl.when(at_end)(lambda: body(2))
+            pl.when(~at_end)(lambda: body(many))
+
+        def late_take():
+            def body(size):
+                for part in range(2):
+                    late_copy(first, size, part).wait_recv()
+                    spread_copy(2, size, part).start()
+                    spread_copy(1, size, part).start()
+                for part in range(2):
+                    spread_copy(2, size, part).wait()
+                    spread_copy(3, size, part).start()
+                for part in range(2):
+                    spread_copy(1, size, part).wait()
+                for part in range(2):
+                    spread_copy(3, size, part).wait()
+
+            by_size(body)
+
+        def late_slot(number):
+            side, lane = lax.div(number, LINE), lax.rem(number, LINE)
+            return parts.at[:, side, :, pl.ds(pl.multiple_of(lane * block, block), block)]
+
+        def late_products():
+            for quarter in range(CHUNKS):
+
+                def body(size):
+                    moved([(r_late.at[quarter, pl.ds(first, size)], blocks.at[pl.ds(0, size)])])
+                    for place in range(size):
+                        late_theirs[place, quarter * rows : (quarter + 1) * rows, :] = blocks[place].astype(LOW)
+
+                by_size(body)
+
+            def product(number, carried):
+                @pl.when((number < 2) | ~at_end)
                 def _():
-                    home = late_home(slot, way)
-                    place = LINE - slot + z if way == 0 else slot - LINE + z
+                    home = late_slot(number)
                     for piece in range(CHUNKS):
-                        home[piece] = late_product(place, piece)
-                    if slot > 1:
-
-                        @pl.when(inner_place(way))
-                        def _():
-                            late_copy(slot - 1, way).wait_recv()
-                            arrived = blocks.at[pl.ds(0, CHUNKS)]
-                            moved([(r_rsd.at[slot - 2, way], arrived)])
-                            home[...] = home[...] + arrived[...]
-
-                    late_copy(slot, way).start()
+                        cut = slice(piece * rows, (piece + 1) * rows)
+                        home[piece] = dot(att_turned[cut, :], late_own[first + number]) + dot(
+                            att_theirs[cut, :], late_theirs[number]
+                        )
+
+                return carried
+
+            lax.fori_loop(0, many, product, 0)
+            for place in range(LINE - 1):
+                pl.when((place == 0) | ~at_end)(lambda: late_pair(place).start())
+
+        def late_pair(place):
+            return remote(late_slot(2 * place + 1 - y), r_dz.at[place], dz_s.at[place], dz_r.at[place], y_peer)
+
+        def late_line(place):
+            goal = lax.div(first, 2) + place
+            return goal != z, remote(late_slot(2 * place + y), r_dx, dx_s.at[place], dx_r, at(z_to=goal))
+
+        def late_sums():
+            for place in range(LINE - 1):
+
+                @pl.when((place == 0) | ~at_end)
+                def _():
+                    late_pair(place).wait()
+                    arrived = blocks.at[pl.ds(0, CHUNKS)]
+                    moved([(r_dz.at[place], arrived)])
+                    home = late_slot(2 * place + y)
+                    home[...] = home[...] + arrived[...]
+                    leaves, copy = late_line(place)
+                    pl.when(leaves)(copy.start)
 
         def late_end():
-            total, arrived = blocks.at[pl.ds(0, CHUNKS)], blocks.at[pl.ds(CHUNKS, CHUNKS)]
+            _, copy = late_line(0)
+            copy.wait_recv()
+            arrived = blocks.at[pl.ds(0, CHUNKS)]
+            moved([(r_dx, arrived)])
+            total = late_slot(2 * (z - lax.div(first, 2)) + y)
             for piece in range(CHUNKS):
-                total[piece] = late_product(z, piece)
-            for way in range(2):
-
-                @pl.when(inner_place(way))
+                gbuf[0:block, piece * rows : (piece + 1) * rows] = (total[piece] + arrived[piece]).T
+            moved([(gbuf.at[pl.ds(0, block)], out_dense)])
+            for place in range(LINE - 1):
+
+                @pl.when((place == 0) | ~at_end)
                 def _():
-                    late_copy(LINE - 1, way).wait_recv()
-                    moved([(r_rsd.at[LINE - 2, way], arrived)])
-                    total[...] = total[...] + arrived[...]
-
-            for piece in range(CHUNKS):
-                gbuf[0:block, piece * rows : (piece + 1) * rows] = total[piece].T
-            moved([(gbuf.at[pl.ds(0, block)], out_dense)])
+                    leaves, copy = late_line(place)
+                    pl.when(leaves)(copy.wait_send)
+
+            for part in range(2):
+                pl.when(at_end)(lambda: late_copy(peer_first, many, part).wait_send())
+                pl.when(~at_end)(lambda: late_copy(peer_first, 2, part).wait_send())
 
         def last_sent():
-            for way in range(2):
-                for slot in range(1, LINE):
-                    pl.when(goes(slot, way))(late_copy(slot, way).wait_send)
-                pl.when(count(way) > 0)(lambda: unit_sent(2 * count(way) - 1, way))
-                pl.when(count(way) > 0)(lambda: unit_sent(2 * count(way) - 2, way))
+            for side in range(2):
+                pl.when(count(toward(side)) > 0)(lambda: unit_sent(2 * count(toward(side)) - 1, side))
+                pl.when(count(toward(side)) > 0)(lambda: unit_sent(2 * count(toward(side)) - 2, side))
 
         def attention_backward(place, carried):
             hot_t = hot_turned[...]
@@ -1127,12 +1206,11 @@
             target, device = ((table_core, core_peer), (table_x, x_peer))[turn]
             return remote(xbuf.at[pl.ds(turn * table_rows, table_rows)], target, table_s.at[turn], table_r.at[turn], device)
 
-        def act_pass():
-            for chunk in range(CHUNKS):
+        def act_pass(chunks):
+            for chunk in chunks:
                 act_take(1, chunk)
                 act_send(2, chunk)
 
-        at_end = (z == 0) | (z == LINE - 1)
 
         for chunk in range(CHUNKS):
             for way in range(2):
@@ -1141,63 +1219,71 @@
         def one_turn(turn, carried):
             for part in range(2):
                 pl.when(turn == 0)(lambda: fetch_units(0, part))
-                unit_slot(turn, part)
+                unit_slot(turn, part, 0)
 
             @pl.when(turn == 0)
             def _():
                 pair_send(1, 0)
                 pair_send(1, 1)
-                for chunk in range(CHUNKS):
-                    act_take(0, chunk)
-                    act_send(1, chunk)
+                act_take(0, CHUNKS - 1)
+                act_send(1, CHUNKS - 1)
+                fetch_rows(r_att, att_theirs)
+                every_chunk(norm_backward)
+                late_send()
+                for step in range(1, LINE):
+                    two_copy(step).wait()
+                for step in range(1, LINE):
+                    two_spread(1, step).start()
+                    two_spread(0, step).start()
 
             @pl.when(turn == 1)
             def _():
-                every_chunk(norm_backward)
                 small_sums()
-                pl.when(~at_end)(act_pass)
-                sums_first()
-                for chunk in range(CHUNKS):
-                    cols_copy(1, chunk).start()
                 pair_send(1, 2)
                 pair_send(1, 3)
-
-            @pl.when(turn == 2)
-            def _():
-                sums_near()
-                for chunk in range(CHUNKS):
-                    cols_copy(1, chunk).wait()
-                fetch_columns(1, late_theirs)
-                fetch_rows(r_att, att_theirs)
-                late_slot(1)
-
-            lately = (turn == 3) & ~at_end | (turn == 2) & at_end
-            pl.when(lately)(lambda: late_slot(2))
-            pl.when((turn == 3) & ~at_end | (turn == 4) & at_end)(down_products)
-            pl.when(lately)(lambda: late_slot(3))
+                pl.when(~at_end)(lambda: act_pass(range(CHUNKS - 1)))
+
+            @pl.when((turn == 1) & ~at_end | (turn == 3) & at_end)
+            def _():
+                late_take()
+                late_products()
+
+            pl.when((turn == 1) & ~at_end)(lambda: act_pass((CHUNKS - 1,)))
+            pl.when(turn == 1)(sums_first)
+
+            pl.when(turn == 2)(sums_near)
+            pl.when((turn == 2) & ~at_end | (turn == 4) & at_end)(late_sums)
 
             @pl.when(turn == 2)
             def _():
                 for part in range(2):
                     fetch_units(1, part)
 
-            @pl.when((turn == 3) & ~at_end | (turn == 5) & at_end)
-            def _():
-                sums_far()
-                sums_middle()
-                down_copy().start()
+            pl.when(turn == 3)(sums_far)
+
+            @pl.when((turn == 3) | (turn == 5))
+            def _():
+                for part in range(2):
+                    unit_slot(jnp.where(turn == 3, 2, 5), part, 1)
+
+            pl.when(turn == 4)(down_products)
+            pl.when((turn == 3) & ~at_end | (turn == 4) & at_end)(sums_middle)
+            pl.when(turn == 4)(lambda: down_copy().start())
 
             @pl.when((turn == 4) & ~at_end | (turn == 5) & at_end)
             def _():
                 sums_end()
                 head_gradients()
+
+            @pl.when(turn == 5)
+            def _():
                 table_part()
+                last_product()
+                unit_end()
 
             return carried
 
         lax.fori_loop(0, 2 * (LINE - 1), one_turn, 0)
-        unit_end()
-        last_product()
         late_end()
         table_middle()
         table_end()
@@ -1208,7 +1294,7 @@
     pl.run_scoped(
         last_scope,
         pltpu.VMEM((3, local_hidden, length), LOW),
-        pltpu.VMEM((LINE, length, block), LOW),
+        pltpu.VMEM((2 * LINE - 2, length, block), LOW),
         pltpu.VMEM((2, length, block), LOW),
         pltpu.VMEM((inner, length), LOW),
         pltpu.VMEM((2, local_hidden, block), FULL),
@@ -1220,7 +1306,7 @@
         pltpu.VMEM(r_sums.shape[1:], FULL),
         pltpu.VMEM(r_sums.shape[1:], FULL),
         pltpu.VMEM(r_sums.shape[1:], FULL),
-        pltpu.VMEM(cols_own.shape, LOW),
+        pltpu.VMEM((2 * LINE, length, block), LOW),
     )
 
 
@@ -1330,15 +1416,17 @@
         ((local_hidden, block), FULL),
         ((8, block), FULL),
         ((LINE, local_hidden, length), FULL),
-        ((LINE, 2, CHUNKS, rows, block), FULL),
+        ((LINE, 2 * CHUNKS, rows, block), FULL),
         ((2, local_hidden, length), FULL),
-        ((2, LINE, CHUNKS, rows, block), FULL),
+        ((LINE, CHUNKS, rows, block), FULL),
         ((inner, length), FULL),
         ((CHUNKS, rows, width), FULL),
         ((CHUNKS, length, inner), FULL),
         ((local_hidden, block), FULL),
         ((2, LINE - 1, 2, local_hidden, block), FULL),
-        ((LINE - 1, 2, CHUNKS, rows, block), FULL),
+        ((4, 2 * LINE, rows, block), FULL),
+        ((LINE - 1, CHUNKS, rows, block), FULL),
+        ((CHUNKS, rows, block), FULL),
         ((4, sums_rows, width // 2), FULL),
     ]
     scratch = [
@@ -1355,10 +1443,10 @@
         ((local_hidden, length), LOW),
         ((2, local_hidden, block), FULL),
         ((LINE, length, block), LOW),
-        ((2, CHUNKS, rows, block), FULL),
+        ((2 * CHUNKS, rows, block), FULL),
         ((LINE, length, block), LOW),
         ((2, length, block), LOW),
-        ((LINE, CHUNKS, rows, block), FULL),
+        ((2 * LINE, rows, block), FULL),
         ((length, inner), LOW),
         ((inner, length), LOW),
         ((3, heads_here, length, HD), LOW),
@@ -1373,9 +1461,9 @@
     dma = pltpu.SemaphoreType.DMA
     each = (3, CHUNKS)
     semaphores = [
-        each, each, each, each, each, each, (2, LINE - 1, CHUNKS), (2, LINE - 1, CHUNKS), each, each, (3,), (3,),
-        (2, CHUNKS), (2, CHUNKS), (2,), (2,), (2, CHUNKS, 2), (2, CHUNKS, 2), None, None, None, None,
-        (3, LINE - 1, 2, 2), (3, LINE - 1, 2, 2), (4,), (4,), (2,), (2,), (4,), (4,),
+        each, each, each, each, each, each, (2, LINE - 1, CHUNKS), (2, LINE - 1, CHUNKS), (3,), (3,), (3, 3), (3, 3),
+        (CHUNKS,), (CHUNKS,), None, None, (2, CHUNKS, 2), (2, CHUNKS, 2), None, None, None, None, (4, 2), (4, 2),
+        (3,), (3,), (3,), None, (2, LINE - 1, 2, 2), (2, LINE - 1, 2, 2), (4,), (4,), (2,), (2,), (4,), (4,),
     ]
     results = pl.pallas_call(
         functools.partial(layer_kernel, length, width, local_hidden),

time: 373 us -> 360 us (0.965)
  Pallas kernels: 367 us -> 356 us
    pallas_call x1, Pallas kernels: 358 us -> 348 us  [local_fast(): pl.pallas_call(functools.partial(layer_kernel, length, width, local_hidde...]
where the time goes in v3:
time: 360 us; the launch traced here: 358 us
  Pallas kernels  356 us (99%)
    pallas_call x1, Pallas kernels, local_fast(): pl.pallas_call(functools.partial(layer_kernel, length, width, local_hidde...  348 us
    pallas_call x1, Pallas kernels, write_out(): pl.pallas_call(write_kernel, out_shape=shapes, in_specs=[hbm] * (len(resu...  8.32 us

profile of v3, /device:TPU:30, one launch (start us, length us, event | category | flops | bytes accessed | tf_op | source)
XLA Modules:
  0.0 357.9 jit_solution(941882316290143185)
XLA Ops:
  1.3 348.1 %shard_map.273 = (bf16[512,2048]{1,0:T(8,128)(2,1)}, f32[16,2048]{1,0:T(8,128)}, f32[256,512]{1,0:T(8,128)}, f32[256,512]{1,0:T(8,128)}, f32[256,512]{1,0:T(8,12...) custom-call(s32[1]{0:T(128)S(6)} %copy.31.prefix_ref, ...), custom_call_target="tpu_custom_call" | custom-call | tf_op jit(solution)/shard_map/pallas_call | solution.py:1468
  349.4 8.3 %shard_map.274 = (bf16[512,2048]{1,0:T(8,128)(2,1)}, f32[16,2048]{1,0:T(8,128)}, f32[256,512]{1,0:T(8,128)}, f32[256,512]{1,0:T(8,128)}, f32[256,512]{1,0:T(8,12...) custom-call(bf16[512,2048]{1,0:T(8,128)(2,1)} %get-tuple-element.37., ...), custom_call_target="tpu_custom_call" | custom-call | tf_op jit(solution)/shard_map/pallas_call | solution.py:1358

commit v4 on v3

--- a/solution.py
+++ b/solution.py
@@ -326,11 +326,11 @@
 
 def layer_kernel(
     length, width, local_hidden,
-    prefix_ref, cluster_ref, ids_row, emb, cos_ref, sin_ref, gain_one, bias_one, gain_two, bias_two, w_query_hbm, w_key_hbm, w_value_hbm, w_dense_hbm,
+    prefix_ref, cluster_ref, ids_row, gain_one, bias_one, gain_two, bias_two, emb_hbm, cos_hbm, sin_hbm, w_query_hbm, w_key_hbm, w_value_hbm, w_dense_hbm,
     w_gate_hbm, w_up_hbm, w_down_hbm, cot_hbm,
     block_out, out_table, out_query, out_key, out_value, out_dense, out_gate, out_up, out_down, out_norms,
     r_act, r_two, r_y, r_cols, r_att, xhat_park, grad_two_park, r_dny, r_rs, r_late, r_dz, r_dx, r_sums,
-    parts, core_in, x_in, back_in, blocks, xbuf, gbuf, obuf, gate_up, grads_low, act_low, send_a, cols_own, cols_send,
+    emb, cos_ref, sin_ref, parts, core_in, x_in, back_in, blocks, xbuf, gbuf, obuf, gate_up, grads_low, act_low, send_a, cols_own, cols_send,
     hidden_theirs, two_own, two_send, att_low, att_turned, heads, w_dense, one_hot, hot_turned, rstd_one, vectors, table_core, table_x,
     core_s, core_r, x_s, x_r, back_s, back_r, act_s, act_r, two_s, two_r, fwd_two_s, fwd_two_r, cols_s, cols_r, fwd_s,
     fwd_r, ys_s, ys_r, att_s, att_r, dny_s, dny_r, late_s, late_r, dz_s, dz_r, dx_s, dx_r, rs_s, rs_r, sums_s, sums_r, table_s, table_r, load_sem, weight_sem,
@@ -477,6 +477,11 @@
 
     other_x = 2 * (1 - x) + core
 
+    def act_pass(chunks):
+        for chunk in chunks:
+            act_take(1, chunk)
+            act_send(2, chunk)
+
     def two_copy(step):
         goal = lax.rem(z + step, LINE)
         return remote(
@@ -542,9 +547,12 @@
             pltpu.make_async_copy(source, target, weight_sem.at[place])
             for place, (source, target) in enumerate(
                 (
+                    (emb_hbm, emb),
                     (w_query_hbm, w_heads.at[0]),
                     (w_key_hbm, w_heads.at[1]),
                     (w_value_hbm, w_heads.at[2]),
+                    (cos_hbm, cos_ref),
+                    (sin_hbm, sin_ref),
                     (w_dense_hbm, w_dense),
                 )
             )
@@ -554,23 +562,27 @@
         named = lax.broadcasted_iota(jnp.int32, (vocab, length), 0) == ids_row[...]
         hot = jnp.where(named, 1.0, 0.0)
         hot_turned[...] = hot.astype(LOW)
-        one_hot[...] = hot.T.astype(LOW)
+        turned_hot = hot.T.astype(LOW)
+        one_hot[:, 0:vocab] = turned_hot
+        one_hot[:, vocab:] = turned_hot
         vectors[...] = jnp.zeros_like(vectors)
+        loads[0].wait()
         for kind in range(3):
-            loads[kind].wait()
-            table = dot(emb[...], w_heads[kind])
+            loads[kind + 1].wait()
+            pieces = split_low(dot(emb[...], w_heads[kind]))
             for place in range(heads_here):
-                tab[kind * heads_here + place] = table[:, place * HD : (place + 1) * HD]
+                for half, piece in enumerate(pieces):
+                    tab[place, half * vocab : (half + 1) * vocab, kind * HD : (kind + 1) * HD] = piece[
+                        :, place * HD : (place + 1) * HD
+                    ]
+        loads[4].wait()
+        loads[5].wait()
 
         def head_inputs(place, carried):
-            hot = one_hot[...]
-            lin = []
-            for kind in range(3):
-                high, rest = split_low(tab[kind * heads_here + place])
-                lin.append(dot(hot, high) + dot(hot, rest))
-            heads[0, place] = turn_by(lin[0], sin_ref[...]).astype(LOW)
-            heads[1, place] = turn_by(lin[1], sin_ref[...]).astype(LOW)
-            heads[2, place] = lin[2].astype(LOW)
+            lin = dot(one_hot[...], tab[place])
+            heads[0, place] = turn_by(lin[:, 0:HD], sin_ref[...]).astype(LOW)
+            heads[1, place] = turn_by(lin[:, HD : 2 * HD], sin_ref[...]).astype(LOW)
+            heads[2, place] = lin[:, 2 * HD :].astype(LOW)
             return carried
 
         lax.fori_loop(0, heads_here, head_inputs, 0)
@@ -587,7 +599,7 @@
 
         def project(chunk):
             attend(chunk)
-            pl.when(chunk == 0)(lambda: loads[3].wait())
+            pl.when(chunk == 0)(lambda: loads[6].wait())
             pl.when(chunk == 0)(lambda: pl.semaphore_wait(barrier, len(greeted)))
             mixed = att_low[chunk_rows(chunk), :]
 
@@ -596,12 +608,13 @@
 
             spread(width, columns, 256)
             core_copy(0, chunk).start()
-            pl.when((chunk > 0) & (chunk <= AHEAD))(lambda: send_part(0, chunk - 1))
+            pl.when(chunk == 0)(lambda: send_part(0, 0))
+            pl.when((chunk > 1) & (chunk <= AHEAD))(lambda: send_part(0, chunk - 1))
 
         every_chunk(project)
         rows_copy().start()
 
-    pl.run_scoped(first_scope, pltpu.VMEM((3, width, inner), LOW), pltpu.VMEM((3 * heads_here, vocab, HD), FULL))
+    pl.run_scoped(first_scope, pltpu.VMEM((3, width, inner), LOW), pltpu.VMEM((heads_here, 2 * vocab, 3 * HD), LOW))
 
     def middle_scope(w_gate, w_up, w_down, cotbuf):
         weight_copies = [
@@ -615,7 +628,7 @@
 
         def feed_forward(chunk):
             branch = take_part(0, chunk)
-            residual = alpha * dot(one_hot[chunk_rows(chunk), :], emb[...]) + branch
+            residual = alpha * dot(one_hot[chunk_rows(chunk), 0:vocab], emb[...]) + branch
             centered = residual - row_mean(residual)
             rstd = lax.rsqrt(row_mean(centered * centered) + norm_eps)
             xhat = centered * rstd
@@ -731,14 +744,16 @@
 
         def step(turn, carried):
             pl.when(turn == CHUNKS - 1)(lambda: hidden_part(0))
+            @pl.when(turn >= 3)
+            def _():
+                act_take(0, turn - 3)
+                act_send(1, turn - 3)
+
             @pl.when(turn == CHUNKS)
             def _():
                 for chunk in range(2):
                     send_part(2, chunk)
                 take_hidden()
-                for chunk in range(CHUNKS - 1):
-                    act_take(0, chunk)
-                    act_send(1, chunk)
 
             pl.when(turn < CHUNKS)(lambda: feed_forward(turn))
             pl.when(turn == 1)(lambda: rows_copy().wait())
@@ -750,6 +765,9 @@
         hidden_part(1)
         for chunk in range(2, CHUNKS):
             send_part(2, chunk)
+        act_take(0, 2)
+        act_send(1, 2)
+        pl.when(~at_end)(lambda: act_pass((0,)))
 
     pl.run_scoped(
         middle_scope,
@@ -1206,20 +1224,21 @@
             target, device = ((table_core, core_peer), (table_x, x_peer))[turn]
             return remote(xbuf.at[pl.ds(turn * table_rows, table_rows)], target, table_s.at[turn], table_r.at[turn], device)
 
-        def act_pass(chunks):
-            for chunk in chunks:
-                act_take(1, chunk)
-                act_send(2, chunk)
-
 
         for chunk in range(CHUNKS):
             for way in range(2):
                 active, copy = act_copy(way, 0, chunk)
                 pl.when(active)(copy.wait_send)
         def one_turn(turn, carried):
+            @pl.when((turn == 2) & at_end)
+            def _():
+                for part in range(2):
+                    fetch_units(1, part)
+
+            swapped = jnp.where(at_end & ((turn == 2) | (turn == 3)), 5 - turn, turn)
             for part in range(2):
                 pl.when(turn == 0)(lambda: fetch_units(0, part))
-                unit_slot(turn, part, 0)
+                pl.when((turn < 4) | (turn == 4) & ~at_end)(lambda: unit_slot(swapped, part, 0))
 
             @pl.when(turn == 0)
             def _():
@@ -1230,6 +1249,7 @@
                 fetch_rows(r_att, att_theirs)
                 every_chunk(norm_backward)
                 late_send()
+                pl.when(~at_end)(lambda: act_pass((1,)))
                 for step in range(1, LINE):
                     two_copy(step).wait()
                 for step in range(1, LINE):
@@ -1241,42 +1261,46 @@
                 small_sums()
                 pair_send(1, 2)
                 pair_send(1, 3)
-                pl.when(~at_end)(lambda: act_pass(range(CHUNKS - 1)))
 
             @pl.when((turn == 1) & ~at_end | (turn == 3) & at_end)
             def _():
                 late_take()
                 late_products()
 
-            pl.when((turn == 1) & ~at_end)(lambda: act_pass((CHUNKS - 1,)))
+            pl.when((turn == 1) & ~at_end)(lambda: act_pass((2, 3)))
             pl.when(turn == 1)(sums_first)
 
             pl.when(turn == 2)(sums_near)
             pl.when((turn == 2) & ~at_end | (turn == 4) & at_end)(late_sums)
 
-            @pl.when(turn == 2)
+            @pl.when((turn == 2) & ~at_end)
             def _():
                 for part in range(2):
                     fetch_units(1, part)
 
-            pl.when(turn == 3)(sums_far)
-
-            @pl.when((turn == 3) | (turn == 5))
+
+            pl.when(turn == 4)(sums_far)
+
+            @pl.when(turn >= 4)
             def _():
                 for part in range(2):
-                    unit_slot(jnp.where(turn == 3, 2, 5), part, 1)
+                    unit_slot(jnp.where(turn == 4, 2, 5), part, 1)
+
+            pl.when((turn == 4) & ~at_end)(sums_middle)
 
             pl.when(turn == 4)(down_products)
-            pl.when((turn == 3) & ~at_end | (turn == 4) & at_end)(sums_middle)
+            pl.when((turn == 4) & at_end)(sums_middle)
             pl.when(turn == 4)(lambda: down_copy().start())
+
+            @pl.when((turn == 4) & at_end | (turn == 5))
+            def _():
+                for part in range(2):
+                    unit_slot(turn, part, 0)
 
             @pl.when((turn == 4) & ~at_end | (turn == 5) & at_end)
             def _():
                 sums_end()
                 head_gradients()
-
-            @pl.when(turn == 5)
-            def _():
                 table_part()
                 last_product()
                 unit_end()
@@ -1430,6 +1454,9 @@
         ((4, sums_rows, width // 2), FULL),
     ]
     scratch = [
+        ((vocab, width), LOW),
+        ((length, HD), FULL),
+        ((length, HD), FULL),
         ((CHUNKS, 2, rows, width // 2), FULL),
         ((CHUNKS, rows, width // 2), FULL),
         ((2, CHUNKS, rows, width // 2), FULL),
@@ -1451,7 +1478,7 @@
         ((inner, length), LOW),
         ((3, heads_here, length, HD), LOW),
         ((width, inner), LOW),
-        ((length, vocab), LOW),
+        ((length, 2 * vocab), LOW),
         ((vocab, length), LOW),
         ((CHUNKS, rows, 1), FULL),
         ((8, width), FULL),
@@ -1463,12 +1490,12 @@
     semaphores = [
         each, each, each, each, each, each, (2, LINE - 1, CHUNKS), (2, LINE - 1, CHUNKS), (3,), (3,), (3, 3), (3, 3),
         (CHUNKS,), (CHUNKS,), None, None, (2, CHUNKS, 2), (2, CHUNKS, 2), None, None, None, None, (4, 2), (4, 2),
-        (3,), (3,), (3,), None, (2, LINE - 1, 2, 2), (2, LINE - 1, 2, 2), (4,), (4,), (2,), (2,), (4,), (4,),
+        (3,), (3,), (3,), None, (2, LINE - 1, 2, 2), (2, LINE - 1, 2, 2), (4,), (4,), (2,), (2,), (4,), (7,),
     ]
     results = pl.pallas_call(
         functools.partial(layer_kernel, length, width, local_hidden),
         out_shape=[jax.ShapeDtypeStruct(shape, dtype) for shape, dtype in shapes],
-        in_specs=[smem] * 2 + [vmem] * 8 + [hbm] * 8,
+        in_specs=[smem] * 2 + [vmem] * 5 + [hbm] * 11,
         out_specs=[hbm] * len(shapes),
         scratch_shapes=[pltpu.VMEM(shape, dtype) for shape, dtype in scratch]
         + [dma if shape is None else dma(shape) for shape in semaphores],
@@ -1479,10 +1506,10 @@
         prefix_lengths,
         cluster_ids,
         token_ids.reshape(1, length),
+        *norms,
         embedding,
         cosine,
         sine,
-        *norms,
         w_query,
         w_key,
         w_value,

time: 360 us -> 355 us (0.986)
  Pallas kernels: 356 us -> 349 us
    pallas_call x1, Pallas kernels: 348 us -> 340 us  [local_fast(): pl.pallas_call(functools.partial(layer_kernel, length, width, local_hidde...]
where the time goes in v4:
time: 355 us; the launch traced here: 350 us
  Pallas kernels  349 us (98%)
    pallas_call x1, Pallas kernels, local_fast(): pl.pallas_call(functools.partial(layer_kernel, length, width, local_hidde...  340 us
    pallas_call x1, Pallas kernels, write_out(): pl.pallas_call(write_kernel, out_shape=shapes, in_specs=[hbm] * (len(resu...  8.32 us

profile of v4, /device:TPU:30, one launch (start us, length us, event | category | flops | bytes accessed | tf_op | source)
XLA Modules:
  0.0 350.0 jit_solution(8827547988455771017)
XLA Ops:
  1.3 340.2 %shard_map.273 = (bf16[512,2048]{1,0:T(8,128)(2,1)}, f32[16,2048]{1,0:T(8,128)}, f32[256,512]{1,0:T(8,128)}, f32[256,512]{1,0:T(8,128)}, f32[256,512]{1,0:T(8,12...) custom-call(s32[1]{0:T(128)S(6)} %copy.31.prefix_ref, ...), custom_call_target="tpu_custom_call" | custom-call | tf_op jit(solution)/shard_map/pallas_call | solution.py:1495
  341.5 8.3 %shard_map.274 = (bf16[512,2048]{1,0:T(8,128)(2,1)}, f32[16,2048]{1,0:T(8,128)}, f32[256,512]{1,0:T(8,128)}, f32[256,512]{1,0:T(8,128)}, f32[256,512]{1,0:T(8,12...) custom-call(bf16[512,2048]{1,0:T(8,128)(2,1)} %get-tuple-element.37., ...), custom_call_target="tpu_custom_call" | custom-call | tf_op jit(solution)/shard_map/pallas_call | solution.py:1382

commit v5 on v4

--- a/solution.py
+++ b/solution.py
@@ -331,7 +331,7 @@
     block_out, out_table, out_query, out_key, out_value, out_dense, out_gate, out_up, out_down, out_norms,
     r_act, r_two, r_y, r_cols, r_att, xhat_park, grad_two_park, r_dny, r_rs, r_late, r_dz, r_dx, r_sums,
     emb, cos_ref, sin_ref, parts, core_in, x_in, back_in, blocks, xbuf, gbuf, obuf, gate_up, grads_low, act_low, send_a, cols_own, cols_send,
-    hidden_theirs, two_own, two_send, att_low, att_turned, heads, w_dense, one_hot, hot_turned, rstd_one, vectors, table_core, table_x,
+    hidden_theirs, gate_theirs, two_own, two_send, att_low, att_turned, heads, w_dense, one_hot, hot_turned, rstd_one, vectors, table_core, table_x, room,
     core_s, core_r, x_s, x_r, back_s, back_r, act_s, act_r, two_s, two_r, fwd_two_s, fwd_two_r, cols_s, cols_r, fwd_s,
     fwd_r, ys_s, ys_r, att_s, att_r, dny_s, dny_r, late_s, late_r, dz_s, dz_r, dx_s, dx_r, rs_s, rs_r, sums_s, sums_r, table_s, table_r, load_sem, weight_sem,
 ):
@@ -343,8 +343,10 @@
     inner = heads_here * HD
     vocab = emb.shape[0]
     shift = (local_hidden + 15) // 16 * 16
-    near = (local_hidden // 2 + 15) // 16 * 16
-    spans = ((0, near), (near, local_hidden - near))
+    quarter = (local_hidden // 4 + 15) // 16 * 16
+    spans = [(start, min(quarter, local_hidden - start)) for start in range(0, local_hidden, quarter)]
+    whole = range(len(spans))
+    halves = ((0, 2 * quarter), (2 * quarter, local_hidden - 2 * quarter))
     block = width // (2 * LINE)
     alpha = jnp.float32(deep_alpha)
 
@@ -475,7 +477,11 @@
             _, copy = act_copy(way, hop, chunk)
             pl.when(act_landed(way, hop))(copy.wait_recv)
 
-    other_x = 2 * (1 - x) + core
+    def chunk_of(place):
+        return jnp.where(place == 0, 0, jnp.where(place == 1, CHUNKS - 1, place - 1))
+
+    mine = chunk_of(mp)
+    other_x = chunk_of(2 * (1 - x) + core)
 
     def act_pass(chunks):
         for chunk in chunks:
@@ -485,12 +491,12 @@
     def two_copy(step):
         goal = lax.rem(z + step, LINE)
         return remote(
-            two_send.at[pl.ds(2 * goal, 2)], r_two.at[z, pl.ds(2 * mp, 2)],
+            two_send.at[pl.ds(2 * goal, 2)], r_two.at[z, pl.ds(2 * mine, 2)],
             two_s.at[step - 1], two_r.at[step - 1], at(z_to=goal),
         )
 
     def two_spread(turn, step):
-        quarter = other_x if turn == 2 else mp
+        quarter = other_x if turn == 2 else mine
         view = r_two.at[lax.rem(z + step, LINE), pl.ds(2 * quarter, 2)]
         device = x_peer if turn == 1 else core_peer
         return remote(view, view, fwd_two_s.at[turn, step - 1], fwd_two_r.at[turn, step - 1], device)
@@ -503,7 +509,7 @@
         )
 
     def pair_send(which, chunk):
-        for part in range(2):
+        for part in whole:
             pair_copy(which, chunk, part).start()
 
     def rows_copy():
@@ -521,6 +527,32 @@
                 for chunk in range(CHUNKS):
                     piece = blocks[CHUNKS * place + chunk].astype(LOW)
                     target[2 * pair + place, chunk * rows : (chunk + 1) * rows, :] = piece
+
+    def toward(side):
+        return jnp.where(z < LINE // 2, side, 1 - side)
+
+    def goes(slot, way):
+        return jnp.where(way == 0, z < slot, z > LINE - 1 - slot)
+
+    def inner_place(way):
+        return jnp.where(way == 0, z > 0, z < LINE - 1)
+
+    def line_goal(way):
+        return at(z_to=jnp.clip(z + 1 - 2 * way, 0, LINE - 1))
+
+    def first_copy(part):
+        way = toward(0)
+        units = pl.ds(*spans[part])
+        return remote(
+            send_a.at[0, units], r_rs.at[0, 0, way, units], rs_s.at[0, 0, way, part], rs_r.at[0, 0, way, part],
+            line_goal(way),
+        )
+
+    def act_sent(chunks):
+        for chunk in chunks:
+            for way in range(2):
+                active, copy = act_copy(way, 0, chunk)
+                pl.when(active)(copy.wait_send)
 
     def every_chunk(body):
         lax.fori_loop(0, CHUNKS, lambda chunk, carried: (body(chunk), carried)[1], 0)
@@ -702,7 +734,7 @@
             for place in range(2):
                 two_own[place, chunk_rows(chunk), :] = blocks[2 * z + place].astype(LOW)
 
-            @pl.when(chunk == mp)
+            @pl.when(chunk == mine)
             def _():
                 two_send[...] = blocks[...]
                 for step in range(1, LINE):
@@ -754,6 +786,12 @@
                 for chunk in range(2):
                     send_part(2, chunk)
                 take_hidden()
+                act_sent(range(2))
+                for chunk in range(2):
+                    for part in whole:
+                        pair_copy(0, chunk, part).wait()
+                moved([(r_y.at[0, :, pl.ds(0, block)], send_a.at[0])])
+                gate_theirs[:, 0:block] = send_a[0].astype(LOW)
 
             pl.when(turn < CHUNKS)(lambda: feed_forward(turn))
             pl.when(turn == 1)(lambda: rows_copy().wait())
@@ -762,9 +800,28 @@
 
         lax.fori_loop(0, CHUNKS + 1, step, 0)
 
+        for chunk in range(CHUNKS - 1):
+            pair_send(1, chunk)
         hidden_part(1)
         for chunk in range(2, CHUNKS):
             send_part(2, chunk)
+        for part in whole:
+            for chunk in range(2, CHUNKS):
+                pair_copy(0, chunk, part).wait()
+            start, size = spans[part]
+            cut = slice(start, start + size)
+            arrived = room.at[pl.ds(0, size)]
+            moved([(r_y.at[0, pl.ds(start, size), pl.ds(block, block)], arrived)])
+            gate_theirs[cut, block:] = arrived[...].astype(LOW)
+
+            @pl.when(at_end)
+            def _():
+                place = jnp.where(z == 0, LINE - 1, 0)
+                send_a[0, cut, :] = dot(grads_low[cut, :], cols_own[place]) + dot(
+                    gate_theirs[cut, :], hidden_theirs[place]
+                )
+                first_copy(part).start()
+
         act_take(0, 2)
         act_send(1, 2)
         pl.when(~at_end)(lambda: act_pass((0,)))
@@ -798,25 +855,21 @@
             for place in range(2 * LINE):
                 late_own[place, chunk_rows(chunk), :] = blocks[place].astype(LOW)
 
-            @pl.when(chunk == mp)
+            @pl.when(chunk == mine)
             def _():
                 for place in range(2 * LINE):
                     cols_send[place] = blocks[place]
+                late_send()
 
             grad_mixed = dot(grad_low, w_dense[...]).astype(LOW)
             for place in range(heads_here):
                 grad_att[place, chunk_rows(chunk), :] = grad_mixed[:, place * HD : (place + 1) * HD]
 
-        def fetch_units(which, part):
-            start, size = spans[part]
+        def fetch_up():
             for chunk in range(CHUNKS):
-                pair_copy(which, chunk, part).wait()
-            views = [stage.at[side, pl.ds(start, size)] for side in range(2)]
-            moved(
-                [(r_y.at[which, pl.ds(start, size), pl.ds(block * side, block)], views[side]) for side in range(2)]
-            )
-            for side in range(2):
-                theirs[1 + which, start : start + size, block * side : block * (side + 1)] = views[side][...].astype(LOW)
+                for part in whole:
+                    pair_copy(1, chunk, part).wait()
+            fetch_rows(r_y.at[1], theirs.at[1])
 
         def fetch_rows(source, target):
             size = source.shape[0]
@@ -830,7 +883,7 @@
 
             def rows_tile(start, size):
                 cut = pl.ds(start, size)
-                target[cut, :] = dot(own[cut, :], right) + dot(other[cut, :], right_theirs)
+                target[cut, :] = dot(own[cut, :], right) + dot(other(cut), right_theirs)
 
             tiles(target.shape[0], rows_tile)
 
@@ -878,20 +931,15 @@
                         active, copy = act_copy(way, hop, chunk)
                         pl.when(active)(copy.wait_send)
 
-        def toward(side):
-            return jnp.where(z < LINE // 2, side, 1 - side)
-
-        def goes(slot, way):
-            return jnp.where(way == 0, z < slot, z > LINE - 1 - slot)
-
-        def inner_place(way):
-            return jnp.where(way == 0, z > 0, z < LINE - 1)
-
-        def line_goal(way):
-            return at(z_to=jnp.clip(z + 1 - 2 * way, 0, LINE - 1))
-
         def unit_terms(kind):
-            return grads_low.at[pl.ds(pl.multiple_of(kind * shift, 16), local_hidden)], theirs.at[1 + kind]
+            own = grads_low.at[pl.ds(pl.multiple_of(kind * shift, 16), local_hidden)]
+
+            def other(cut):
+                if isinstance(kind, int):
+                    return theirs[1, cut, :] if kind else gate_theirs[cut, :]
+                return jnp.where(kind == 0, gate_theirs[cut, :], theirs[1, cut, :])
+
+            return own, other
 
         def count(way):
             return jnp.where(way == 0, LINE - 1 - z, z)
@@ -906,7 +954,7 @@
         def unit_copy(turn, side, part):
             way = toward(side)
             kind, slot = lax.div(turn, LINE - 1), lax.rem(turn, LINE - 1)
-            units = pl.ds(*spans[part])
+            units = pl.ds(*halves[part])
             home = (send_a, send_b)[side].at[lax.rem(jnp.maximum(order(kind, slot + 1, way), 0), 2), units]
             return remote(
                 home, r_rs.at[kind, slot, way, units], rs_s.at[kind, slot, way, part], rs_r.at[kind, slot, way, part],
@@ -914,14 +962,23 @@
             )
 
         def unit_sent(number, side):
-            for part in range(2):
-                unit_copy(turn_of(jnp.maximum(number, 0), toward(side)), side, part).wait_send()
+            turn = turn_of(jnp.maximum(number, 0), toward(side))
+
+            @pl.when(turn == 0)
+            def _():
+                for part in whole:
+                    first_copy(part).wait_send()
+
+            @pl.when(turn > 0)
+            def _():
+                for part in range(2):
+                    unit_copy(turn, side, part).wait_send()
 
         def unit_slot(turn, part, side):
             way = toward(side)
             kind, slot = lax.div(turn, LINE - 1), lax.rem(turn, LINE - 1) + 1
             own, other = unit_terms(kind)
-            start, size = spans[part]
+            start, size = halves[part]
             cut = slice(start, start + size)
 
             @pl.when(goes(slot, way))
@@ -931,12 +988,18 @@
                 if part == 0:
                     pl.when(number >= 2)(lambda: unit_sent(number - 2, side))
                 place = jnp.where(way == 0, LINE - slot + z, slot - LINE + z)
-                home[cut, :] = dot(own[cut, :], cols_own[place]) + dot(other[cut, :], hidden_theirs[place])
+                home[cut, :] = dot(own[cut, :], cols_own[place]) + dot(other(cut), hidden_theirs[place])
 
                 @pl.when((slot > 1) & inner_place(way))
                 def _():
                     before = jnp.maximum(turn - 1, 0)
-                    unit_copy(before, side, part).wait_recv()
+
+                    @pl.when(before == 0)
+                    def _():
+                        for piece in (2 * part, 2 * part + 1):
+                            first_copy(piece).wait_recv()
+
+                    pl.when(before > 0)(lambda: unit_copy(before, side, part).wait_recv())
                     landed = r_rs.at[lax.div(before, LINE - 1), lax.rem(before, LINE - 1), way, pl.ds(start, size)]
                     moved([(landed, stage.at[side, pl.ds(start, size)])])
                     home[cut, :] = home[cut, :] + stage[side, cut, :]
@@ -972,7 +1035,7 @@
         many = 2 * LINE - 2
         def late_copy(begin, size, part):
             span = pl.ds(begin + part * (size // 2), size // 2)
-            return remote(cols_send.at[span], r_late.at[mp, span], late_s.at[0, part], late_r.at[0, part], z_peer)
+            return remote(cols_send.at[span], r_late.at[mine, span], late_s.at[0, part], late_r.at[0, part], z_peer)
 
         def late_send():
             for part in range(2):
@@ -980,7 +1043,7 @@
                 pl.when(~at_end)(lambda: late_copy(peer_first, 2, part).start())
 
         def spread_copy(turn, size, part):
-            place = other_x if turn == 3 else mp
+            place = other_x if turn == 3 else mine
             view = r_late.at[place, pl.ds(first + part * (size // 2), size // 2)]
             device = x_peer if turn == 2 else core_peer
             return remote(view, view, late_s.at[turn, part], late_r.at[turn, part], device)
@@ -1225,30 +1288,22 @@
             return remote(xbuf.at[pl.ds(turn * table_rows, table_rows)], target, table_s.at[turn], table_r.at[turn], device)
 
 
-        for chunk in range(CHUNKS):
-            for way in range(2):
-                active, copy = act_copy(way, 0, chunk)
-                pl.when(active)(copy.wait_send)
         def one_turn(turn, carried):
             @pl.when((turn == 2) & at_end)
             def _():
-                for part in range(2):
-                    fetch_units(1, part)
+                fetch_up()
 
             swapped = jnp.where(at_end & ((turn == 2) | (turn == 3)), 5 - turn, turn)
             for part in range(2):
-                pl.when(turn == 0)(lambda: fetch_units(0, part))
-                pl.when((turn < 4) | (turn == 4) & ~at_end)(lambda: unit_slot(swapped, part, 0))
+                pl.when((turn > 0) & (turn < 4) | (turn == 4) & ~at_end)(lambda: unit_slot(swapped, part, 0))
 
             @pl.when(turn == 0)
             def _():
-                pair_send(1, 0)
-                pair_send(1, 1)
                 act_take(0, CHUNKS - 1)
                 act_send(1, CHUNKS - 1)
                 fetch_rows(r_att, att_theirs)
                 every_chunk(norm_backward)
-                late_send()
+                act_sent(range(2, CHUNKS))
                 pl.when(~at_end)(lambda: act_pass((1,)))
                 for step in range(1, LINE):
                     two_copy(step).wait()
@@ -1259,8 +1314,7 @@
             @pl.when(turn == 1)
             def _():
                 small_sums()
-                pair_send(1, 2)
-                pair_send(1, 3)
+                pair_send(1, CHUNKS - 1)
 
             @pl.when((turn == 1) & ~at_end | (turn == 3) & at_end)
             def _():
@@ -1275,33 +1329,46 @@
 
             @pl.when((turn == 2) & ~at_end)
             def _():
+                fetch_up()
+
+
+            pl.when(turn == 4)(sums_far)
+
+            @pl.when(turn == 4)
+            def _():
                 for part in range(2):
-                    fetch_units(1, part)
-
-
-            pl.when(turn == 4)(sums_far)
-
-            @pl.when(turn >= 4)
-            def _():
-                for part in range(2):
-                    unit_slot(jnp.where(turn == 4, 2, 5), part, 1)
+                    unit_slot(2, part, 1)
 
             pl.when((turn == 4) & ~at_end)(sums_middle)
-
             pl.when(turn == 4)(down_products)
-            pl.when((turn == 4) & at_end)(sums_middle)
-            pl.when(turn == 4)(lambda: down_copy().start())
-
-            @pl.when((turn == 4) & at_end | (turn == 5))
-            def _():
-                for part in range(2):
-                    unit_slot(turn, part, 0)
-
-            @pl.when((turn == 4) & ~at_end | (turn == 5) & at_end)
-            def _():
+
+            @pl.when((turn == 4) & ~at_end)
+            def _():
+                down_copy().start()
                 sums_end()
                 head_gradients()
-                table_part()
+
+            @pl.when((turn == 4) & at_end)
+            def _():
+                for part in range(2):
+                    unit_slot(4, part, 0)
+                sums_middle()
+                down_copy().start()
+
+            @pl.when(turn == 5)
+            def _():
+                for part in range(2):
+                    for side in range(2):
+                        unit_slot(5, part, side)
+                    if part == 0:
+                        pl.when(~at_end)(table_part)
+
+                @pl.when(at_end)
+                def _():
+                    sums_end()
+                    head_gradients()
+                    table_part()
+
                 last_product()
                 unit_end()
 
@@ -1317,7 +1384,7 @@
 
     pl.run_scoped(
         last_scope,
-        pltpu.VMEM((3, local_hidden, length), LOW),
+        pltpu.VMEM((2, local_hidden, length), LOW),
         pltpu.VMEM((2 * LINE - 2, length, block), LOW),
         pltpu.VMEM((2, length, block), LOW),
         pltpu.VMEM((inner, length), LOW),
@@ -1472,6 +1539,7 @@
         ((LINE, length, block), LOW),
         ((2 * CHUNKS, rows, block), FULL),
         ((LINE, length, block), LOW),
+        ((local_hidden, length), LOW),
         ((2, length, block), LOW),
         ((2 * LINE, rows, block), FULL),
         ((length, inner), LOW),
@@ -1484,13 +1552,14 @@
         ((8, width), FULL),
         ((table_rows, width), FULL),
         ((table_rows, width), FULL),
+        (((local_hidden // 4 + 15) // 16 * 16, block), FULL),
     ]
     dma = pltpu.SemaphoreType.DMA
     each = (3, CHUNKS)
     semaphores = [
         each, each, each, each, each, each, (2, LINE - 1, CHUNKS), (2, LINE - 1, CHUNKS), (3,), (3,), (3, 3), (3, 3),
-        (CHUNKS,), (CHUNKS,), None, None, (2, CHUNKS, 2), (2, CHUNKS, 2), None, None, None, None, (4, 2), (4, 2),
-        (3,), (3,), (3,), None, (2, LINE - 1, 2, 2), (2, LINE - 1, 2, 2), (4,), (4,), (2,), (2,), (4,), (7,),
+        (CHUNKS,), (CHUNKS,), None, None, (2, CHUNKS, 4), (2, CHUNKS, 4), None, None, None, None, (4, 2), (4, 2),
+        (3,), (3,), (3,), None, (2, LINE - 1, 2, 4), (2, LINE - 1, 2, 4), (4,), (4,), (2,), (2,), (4,), (7,),
     ]
     results = pl.pallas_call(
         functools.partial(layer_kernel, length, width, local_hidden),

time: 355 us -> 351 us (0.989)
  no operation moved by 1% of the time
where the time goes in v5:
time: 351 us; the launch traced here: 349 us
  Pallas kernels  348 us (99%)
    pallas_call x1, Pallas kernels, local_fast(): pl.pallas_call(functools.partial(layer_kernel, length, width, local_hidde...  340 us
    pallas_call x1, Pallas kernels, write_out(): pl.pallas_call(write_kernel, out_shape=shapes, in_specs=[hbm] * (len(resu...  8.32 us

profile of v5, /device:TPU:30, one launch (start us, length us, event | category | flops | bytes accessed | tf_op | source)
XLA Modules:
  0.0 349.3 jit_solution(6568810939344756284)
XLA Ops:
  1.3 339.6 %shard_map.273 = (bf16[512,2048]{1,0:T(8,128)(2,1)}, f32[16,2048]{1,0:T(8,128)}, f32[256,512]{1,0:T(8,128)}, f32[256,512]{1,0:T(8,128)}, f32[256,512]{1,0:T(8,12...) custom-call(s32[1]{0:T(128)S(6)} %copy.31.prefix_ref, ...), custom_call_target="tpu_custom_call" | custom-call | tf_op jit(solution)/shard_map/pallas_call | solution.py:1564
  340.9 8.3 %shard_map.274 = (bf16[512,2048]{1,0:T(8,128)(2,1)}, f32[16,2048]{1,0:T(8,128)}, f32[256,512]{1,0:T(8,128)}, f32[256,512]{1,0:T(8,128)}, f32[256,512]{1,0:T(8,12...) custom-call(bf16[512,2048]{1,0:T(8,128)(2,1)} %get-tuple-element.37., ...), custom_call_target="tpu_custom_call" | custom-call | tf_op jit(solution)/shard_map/pallas_call | solution.py:1449

commit v6 on v5

--- a/solution.py
+++ b/solution.py
@@ -285,7 +285,7 @@
 LINE = 4
 MESH = pl.DeviceIdType.MESH
 CHUNKS = 4
-AHEAD = 2
+AHEAD = 3
 LOW = jnp.bfloat16
 FULL = jnp.float32
 TANH_SCALE = math.sqrt(2.0 / math.pi)
@@ -774,14 +774,16 @@
                 cols_copy(chunk).wait()
             fetch_columns(hidden_theirs)
 
+        lag = AHEAD - 1
+
         def step(turn, carried):
-            pl.when(turn == CHUNKS - 1)(lambda: hidden_part(0))
+            pl.when(turn == CHUNKS - 2 + lag)(lambda: hidden_part(0))
             @pl.when(turn >= 3)
             def _():
                 act_take(0, turn - 3)
                 act_send(1, turn - 3)
 
-            @pl.when(turn == CHUNKS)
+            @pl.when(turn == CHUNKS - 1 + lag)
             def _():
                 for chunk in range(2):
                     send_part(2, chunk)
@@ -794,11 +796,11 @@
                 gate_theirs[:, 0:block] = send_a[0].astype(LOW)
 
             pl.when(turn < CHUNKS)(lambda: feed_forward(turn))
-            pl.when(turn == 1)(lambda: rows_copy().wait())
-            pl.when(turn > 0)(lambda: feed_backward(turn - 1))
+            pl.when(turn == lag)(lambda: rows_copy().wait())
+            pl.when(turn >= lag)(lambda: feed_backward(turn - lag))
             return carried
 
-        lax.fori_loop(0, CHUNKS + 1, step, 0)
+        lax.fori_loop(0, CHUNKS + lag, step, 0)
 
         for chunk in range(CHUNKS - 1):
             pair_send(1, chunk)
@@ -822,8 +824,6 @@
                 )
                 first_copy(part).start()
 
-        act_take(0, 2)
-        act_send(1, 2)
         pl.when(~at_end)(lambda: act_pass((0,)))
 
     pl.run_scoped(

time: 351 us -> 349 us (level)
  Pallas kernels: 348 us -> 343 us
    pallas_call x1, Pallas kernels: 340 us -> 334 us  [local_fast(): pl.pallas_call(functools.partial(layer_kernel, length, width, local_hidde...]
where the time goes in v6:
time: 349 us; the launch traced here: 344 us
  Pallas kernels  343 us (98%)
    pallas_call x1, Pallas kernels, local_fast(): pl.pallas_call(functools.partial(layer_kernel, length, width, local_hidde...  334 us
    pallas_call x1, Pallas kernels, write_out(): pl.pallas_call(write_kernel, out_shape=shapes, in_specs=[hbm] * (len(resu...  8.32 us

profile of v6, /device:TPU:30, one launch (start us, length us, event | category | flops | bytes accessed | tf_op | source)
XLA Modules:
  0.0 344.3 jit_solution(12125613562890345095)
XLA Ops:
  1.3 334.5 %shard_map.273 = (bf16[512,2048]{1,0:T(8,128)(2,1)}, f32[16,2048]{1,0:T(8,128)}, f32[256,512]{1,0:T(8,128)}, f32[256,512]{1,0:T(8,128)}, f32[256,512]{1,0:T(8,12...) custom-call(s32[1]{0:T(128)S(6)} %copy.31.prefix_ref, ...), custom_call_target="tpu_custom_call" | custom-call | tf_op jit(solution)/shard_map/pallas_call | solution.py:1564
  335.8 8.3 %shard_map.274 = (bf16[512,2048]{1,0:T(8,128)(2,1)}, f32[16,2048]{1,0:T(8,128)}, f32[256,512]{1,0:T(8,128)}, f32[256,512]{1,0:T(8,128)}, f32[256,512]{1,0:T(8,12...) custom-call(bf16[512,2048]{1,0:T(8,128)(2,1)} %get-tuple-element.37., ...), custom_call_target="tpu_custom_call" | custom-call | tf_op jit(solution)/shard_map/pallas_call | solution.py:1449

commit v7 on v6

--- a/solution.py
+++ b/solution.py
@@ -1415,13 +1415,14 @@
     more = [
         pltpu.make_async_copy(landed.at[1, LINE - 2, way], terms.at[way], first_sem.at[count + way]) for way in range(2)
     ]
-    for copy in more:
-        copy.start()
+    lands = (z > 0, z < LINE - 1)
+    for way in range(2):
+        pl.when(lands[way])(more[way].start)
     for place in order:
         loads[place].start()
     stores = []
-    for copy in more:
-        copy.wait()
+    for way in range(2):
+        pl.when(lands[way])(more[way].wait)
     for place in order:
         loads[place].wait()
         room = rooms[place]

time: 349 us -> 349 us (level)
  no operation moved by 1% of the time
where the time goes in v7:
time: 349 us; the launch traced here: 344 us
  Pallas kernels  342 us (98%)
    pallas_call x1, Pallas kernels, local_fast(): pl.pallas_call(functools.partial(layer_kernel, length, width, local_hidde...  334 us
    pallas_call x1, Pallas kernels, write_out(): pl.pallas_call(write_kernel, out_shape=shapes, in_specs=[hbm] * (len(resu...  7.8 us

profile of v7, /device:TPU:30, one launch (start us, length us, event | category | flops | bytes accessed | tf_op | source)
XLA Modules:
  0.0 343.8 jit_solution(2799734123375762241)
XLA Ops:
  1.3 334.5 %shard_map.273 = (bf16[512,2048]{1,0:T(8,128)(2,1)}, f32[16,2048]{1,0:T(8,128)}, f32[256,512]{1,0:T(8,128)}, f32[256,512]{1,0:T(8,128)}, f32[256,512]{1,0:T(8,12...) custom-call(s32[1]{0:T(128)S(6)} %copy.31.prefix_ref, ...), custom_call_target="tpu_custom_call" | custom-call | tf_op jit(solution)/shard_map/pallas_call | solution.py:1565
  335.8 7.8 %shard_map.274 = (bf16[512,2048]{1,0:T(8,128)(2,1)}, f32[16,2048]{1,0:T(8,128)}, f32[256,512]{1,0:T(8,128)}, f32[256,512]{1,0:T(8,128)}, f32[256,512]{1,0:T(8,12...) custom-call(bf16[512,2048]{1,0:T(8,128)(2,1)} %get-tuple-element.37., ...), custom_call_target="tpu_custom_call" | custom-call | tf_op jit(solution)/shard_map/pallas_call | solution.py:1450
